TPU v7x, 32 devices: a whole 2x2x4 slice. The times are simulated.
32 devices in a mesh: seq: 8 (over z, x), dp: 4 (over y, core).
Axes of the slice: x: 2, y: 2, z: 4, core: 2. Of those that a mesh axis runs over, the one named last changes fastest.
Arguments:
- tokens: bfloat16 [8, 4096, 768], P('dp', 'seq'), may hold values from -6 to 6
- starts: int32 [8, 4096], P('dp', 'seq'), may hold values from 0 to 1, as said below
- cotangent: bfloat16 [8, 4096, 768], P('dp', 'seq'), may hold values from -6 to 6
- in_weight: float32 [768, 3352], P(None, 'dp'), may hold values from -0.21875 to 0.21875
- out_weight: float32 [1536, 768], P('dp'), may hold values from -0.15625 to 0.15625
- vectors: float32 [11336], P('dp'), may hold values from -7 to 2.1
- in_moment: float32 [768, 3352], P(None, 'dp'), may hold values from -320 to 320
- out_moment: float32 [1536, 768], P('dp'), may hold values from -1024 to 1024
- vec_moment1: float32 [11336], P('dp'), may hold values from -32 to 32
- vec_moment2: float32 [11336], P('dp'), may hold values from 154.0096 to 622.592
Outputs:
- block_out: bfloat16 [8, 4096, 768], P('dp', 'seq')
- input_grad: float32 [8, 4096, 768], P('dp', 'seq')
- new_in_moment: float32 [768, 3352], P(None, 'dp')
- new_in_weight: float32 [768, 3352], P(None, 'dp')
- new_out_moment: float32 [1536, 768], P('dp')
- new_out_weight: float32 [1536, 768], P('dp')
- new_vec_moment1: float32 [11336], P('dp')
- new_vec_moment2: float32 [11336], P('dp')
- new_vectors: float32 [11336], P('dp')
Inputs may be any that keep to these rules, and one draw needn't show every extreme that they name: No document starts at position 0 of a packed sequence or in the last 3 positions of any device's block of 512 positions; on each index of dp one of its 2 packed sequences has no start.
All inputs are finite; a program needn't handle non-finite values.
Results may differ from a plain program's by a relative error of at most 0.015.
The roundings to bfloat16 on the way count: a program that leaves them out, or rounds other values in their place, can miss the bound.
Values may be sent and summed in bfloat16 or wider, within the bound.
A program may use at most 512 MiB of HBM per device.

v0:
```python
import jax
import jax.numpy as jnp
from jax import lax
from jax.sharding import PartitionSpec as P

D = 768
H = 24
P_SIZE = 64
N = 128
E = 1536
CONV = 1792
IN = 3352
KW = 4
BLOCK = 256
ITERS = 5
STEP = 10


EPSILON = 1e-05
MOMENTUM = 0.95
NS_A = 3.4445
NS_B = -4.775
NS_C = 2.0315
RATE_MATRIX = 0.5
RATE_VECTOR = 0.2
WEIGHT_DECAY = 0.01
BETA_FIRST = 0.9
BETA_SECOND = 0.95
ADAM_EPSILON = 1e-08
PRECISE = lax.Precision.HIGHEST


def from_behind(x, axis, by):
    devices = lax.axis_size(axis)
    pairs = [(i, i + by) for i in range(devices) if 0 <= i + by < devices]
    return lax.ppermute(x, axis, pairs)


def prefix(x, axis, combine, identity, reverse):
    devices, here = (lax.axis_size(axis), lax.axis_index(axis))
    everything = jax.tree.map(
        lambda part, kind: lax.all_gather(part.astype(kind), axis), x, (jnp.bfloat16, jnp.bfloat16)
    )
    start = jax.tree.map(
        lambda part, zero: jnp.broadcast_to(jnp.asarray(zero, part.dtype), part.shape), x, identity
    )

    def hop(k, before):
        at = devices - 1 - k if reverse else k
        reached = at > here if reverse else at < here
        new = combine(
            before, jax.tree.map(lambda part, own: part[at].astype(own.dtype), everything, x)
        )
        return jax.tree.map(lambda a, b: jnp.where(reached, a, b), new, before)

    return lax.fori_loop(0, devices, hop, start)


def split_vector(packed):
    offset = D + E + CONV
    gain_in = packed[:D]
    gain_out = packed[D : D + E]
    conv_bias = packed[D + E : offset]
    conv_taps = packed[offset : offset + KW * CONV].reshape(KW, CONV)
    offset = offset + KW * CONV
    step_bias = packed[offset : offset + H]
    decay_log = packed[offset + H : offset + 2 * H]
    skip_gain = packed[offset + 2 * H : offset + 3 * H]
    return (gain_in, gain_out, conv_bias, conv_taps, step_bias, decay_log, skip_gain)


def silu_slope(value):
    sigma = jax.nn.sigmoid(value)
    return sigma * (1.0 + value * (1.0 - sigma))


def combine_forward(earlier, later):
    return (earlier[0] * later[0], later[0][..., None, None] * earlier[1] + later[1])


def combine_backward(earlier, later):
    return (later[0] * earlier[0], later[1] + later[0][..., None, None] * earlier[1])


def per_device(
    tokens,
    starts,
    cotangent,
    in_weight,
    out_weight,
    vectors,
    in_moment,
    out_moment,
    vec_moment1,
    vec_moment2,
):
    w_in_low, w_out_low, vec_low = (
        lax.all_gather(in_weight.astype(jnp.bfloat16), "dp", axis=1, tiled=True),
        lax.all_gather(out_weight.astype(jnp.bfloat16), "dp", axis=0, tiled=True),
        lax.all_gather(vectors.astype(jnp.bfloat16), "dp", axis=0, tiled=True),
    )
    gain_in, gain_out, conv_bias, conv_taps, step_bias, decay_log, skip_gain = split_vector(
        vec_low.astype(jnp.float32)
    )
    pack_count = tokens.shape[0]
    local_rows = tokens.shape[1]
    block_count = local_rows // BLOCK
    edge_rows = KW - 1
    shape_blocks = (pack_count, block_count, BLOCK)
    inputs = tokens.astype(jnp.float32)
    inv_rms = lax.rsqrt(jnp.mean(inputs * inputs, -1, keepdims=True) + EPSILON)
    scaled = inputs * inv_rms
    normed = (scaled * gain_in).astype(jnp.bfloat16)
    projected = jnp.dot(normed, w_in_low, preferred_element_type=jnp.float32)
    gate_pre = projected[..., :E]
    conv_input = projected[..., E : E + CONV].astype(jnp.bfloat16)
    step_raw = projected[..., E + CONV :]
    edge = from_behind(conv_input[:, local_rows - edge_rows :, :], "seq", 1)
    extended = jnp.concatenate([edge, conv_input], axis=1).astype(jnp.float32)
    doc_count = jnp.cumsum(starts, axis=1)
    count_ext = jnp.concatenate(
        [jnp.zeros((pack_count, edge_rows), doc_count.dtype), doc_count], axis=1
    )
    tap_keep = [
        (count_ext[:, tap_index : tap_index + local_rows] == doc_count).astype(jnp.float32)[
            ..., None
        ]
        for tap_index in range(KW)
    ]
    conv_pre = conv_bias + extended[:, 0:local_rows] * conv_taps[0] * tap_keep[0]
    for tap_index in range(1, KW):
        conv_pre = (
            conv_pre
            + extended[:, tap_index : tap_index + local_rows]
            * conv_taps[tap_index]
            * tap_keep[tap_index]
        )
    activated = jax.nn.silu(conv_pre)
    step_arg = step_raw + step_bias
    step_size = jax.nn.softplus(step_arg)
    decay_rate = -jnp.exp(decay_log)
    log_decay = step_size * decay_rate
    x_full = activated[..., :E].reshape(shape_blocks + (H, P_SIZE))
    x_low = x_full.astype(jnp.bfloat16)
    b_low = activated[..., E : E + N].reshape(shape_blocks + (N,)).astype(jnp.bfloat16)
    c_low = activated[..., E + N :].reshape(shape_blocks + (N,)).astype(jnp.bfloat16)
    step_blocks = step_size.reshape(shape_blocks + (H,))
    cum_decay = jnp.cumsum(log_decay.reshape(shape_blocks + (H,)), axis=2)
    segment = jnp.cumsum(starts.reshape(shape_blocks), axis=2)
    lower = jnp.arange(BLOCK)[:, None] >= jnp.arange(BLOCK)[None, :]
    pair_mask = (segment[..., :, None] == segment[..., None, :]) & lower
    scores = jnp.einsum("abtn,absn->abts", c_low, b_low, preferred_element_type=jnp.float32)
    cum_heads = jnp.moveaxis(cum_decay, -1, 2)
    pair_gap = cum_heads[..., :, None] - cum_heads[..., None, :]
    pair_decay = jnp.exp(jnp.where(pair_mask[:, :, None], pair_gap, -jnp.inf))
    step_cols = jnp.moveaxis(step_blocks, -1, 2)[..., None, :]
    mix_full = scores[:, :, None] * pair_decay * step_cols
    mix_low = mix_full.astype(jnp.bfloat16)
    y_diag = jnp.einsum("abhts,abshp->abthp", mix_low, x_low, preferred_element_type=jnp.float32)
    end_same = (segment == segment[:, :, -1:]).astype(jnp.float32)[..., None]
    end_decay = jnp.exp(cum_decay[:, :, -1:, :] - cum_decay) * end_same
    end_weight = end_decay * step_blocks
    x_weighted = (x_low.astype(jnp.float32) * end_weight[..., None]).astype(jnp.bfloat16)
    block_state = jnp.einsum(
        "abshp,absn->abhpn", x_weighted, b_low, preferred_element_type=jnp.float32
    )
    block_decay = (
        jnp.exp(cum_decay[:, :, -1, :]) * (segment[:, :, -1] == 0).astype(jnp.float32)[..., None]
    )
    decay_total = block_decay[:, 0]
    state_total = block_state[:, 0]
    block_index = 1
    state_total = (
        block_decay[:, block_index][..., None, None] * state_total + block_state[:, block_index]
    )
    decay_total = decay_total * block_decay[:, block_index]
    entering = prefix(
        (decay_total, state_total),
        "seq",
        combine_forward,
        (jnp.ones_like(decay_total), jnp.zeros_like(state_total)),
        False,
    )[1]
    state_list = [entering]
    block_index = 0
    state_list.append(
        block_decay[:, block_index][..., None, None] * state_list[-1] + block_state[:, block_index]
    )
    state_in = jnp.stack(state_list, axis=1)
    state_low = state_in.astype(jnp.bfloat16)
    y_carry = jnp.einsum("abtn,abhpn->abthp", c_low, state_low, preferred_element_type=jnp.float32)
    carry_scale = jnp.exp(cum_decay) * (segment == 0).astype(jnp.float32)[..., None]
    y_blocks = y_diag + carry_scale[..., None] * y_carry + skip_gain[:, None] * x_full
    mixed = y_blocks.reshape(pack_count, local_rows, E)
    gate_act = jax.nn.silu(gate_pre)
    gated = mixed * gate_act
    inv_gate = lax.rsqrt(jnp.mean(gated * gated, -1, keepdims=True) + EPSILON)
    gated_hat = gated * inv_gate
    gated_low = (gated_hat * gain_out).astype(jnp.bfloat16)
    branch = jnp.dot(gated_low, w_out_low, preferred_element_type=jnp.float32)
    result = (inputs + branch).astype(jnp.bfloat16)
    grad_w_out = jnp.einsum("ate,atd->ed", gated_low, cotangent, preferred_element_type=jnp.float32)
    grad_ghat = jnp.einsum("atd,ed->ate", cotangent, w_out_low, preferred_element_type=jnp.float32)
    grad_gain_out = jnp.sum(grad_ghat * gated_hat, axis=(0, 1))
    grad_scaled_gate = grad_ghat * gain_out
    grad_gated = inv_gate * (
        grad_scaled_gate - gated_hat * jnp.mean(grad_scaled_gate * gated_hat, -1, keepdims=True)
    )
    grad_mixed = grad_gated * gate_act
    grad_gate = grad_gated * mixed * silu_slope(gate_pre)
    grad_y = grad_mixed.reshape(shape_blocks + (H, P_SIZE))
    grad_diag_low = grad_y.astype(jnp.bfloat16)
    grad_carry_low = (carry_scale[..., None] * grad_y).astype(jnp.bfloat16)
    grad_cum = jnp.sum(grad_y * y_carry, -1) * carry_scale
    grad_skip = jnp.sum(grad_y * x_full, axis=(0, 1, 2, 4))
    grad_x = skip_gain[:, None] * grad_y
    grad_mix = jnp.einsum(
        "abthp,abshp->abhts", grad_diag_low, x_low, preferred_element_type=jnp.float32
    )
    grad_x = grad_x + jnp.einsum(
        "abhts,abthp->abshp", mix_low, grad_diag_low, preferred_element_type=jnp.float32
    )
    grad_c = jnp.einsum(
        "abthp,abhpn->abtn", grad_carry_low, state_low, preferred_element_type=jnp.float32
    )
    grad_state_in = jnp.einsum(
        "abthp,abtn->abhpn", grad_carry_low, c_low, preferred_element_type=jnp.float32
    )
    local_adjoint = grad_state_in[:, block_count - 1]
    block_index = 0
    local_adjoint = (
        grad_state_in[:, block_index] + block_decay[:, block_index][..., None, None] * local_adjoint
    )
    adjoint_next = prefix(
        (decay_total, local_adjoint),
        "seq",
        combine_backward,
        (jnp.ones_like(decay_total), jnp.zeros_like(local_adjoint)),
        True,
    )[1]
    state_grads = [None] * block_count
    decay_grads = [None] * block_count
    for block_index in range(block_count - 1, -1, -1):
        state_grads[block_index] = adjoint_next
        decay_grads[block_index] = jnp.sum(adjoint_next * state_in[:, block_index], axis=(-2, -1))
        adjoint_next = (
            grad_state_in[:, block_index]
            + block_decay[:, block_index][..., None, None] * adjoint_next
        )
    grad_state_low = jnp.stack(state_grads, axis=1).astype(jnp.bfloat16)
    grad_block_decay = jnp.stack(decay_grads, axis=1)
    grad_xw = jnp.einsum(
        "abhpn,absn->abshp", grad_state_low, b_low, preferred_element_type=jnp.float32
    )
    grad_b = jnp.einsum(
        "abhpn,abshp->absn", grad_state_low, x_weighted, preferred_element_type=jnp.float32
    )
    grad_x = grad_x + grad_xw * end_weight[..., None]
    grad_end = jnp.sum(grad_xw * x_low.astype(jnp.float32), -1)
    grad_step = grad_end * end_decay
    grad_gap = grad_end * end_weight
    grad_cum = grad_cum - grad_gap
    last_extra = jnp.sum(grad_gap, axis=2) + grad_block_decay * block_decay
    grad_cum = jnp.concatenate(
        [grad_cum[:, :, :-1], grad_cum[:, :, -1:] + last_extra[:, :, None]], axis=2
    )
    product = grad_mix * mix_full
    grad_cum = grad_cum + jnp.moveaxis(jnp.sum(product, -1) - jnp.sum(product, -2), 2, 3)
    grad_step = grad_step + jnp.moveaxis(
        jnp.sum(grad_mix * scores[:, :, None] * pair_decay, axis=3), 2, 3
    )
    grad_scores = jnp.sum(grad_mix * pair_decay * step_cols, axis=2).astype(jnp.bfloat16)
    grad_c = grad_c + jnp.einsum(
        "abts,absn->abtn", grad_scores, b_low, preferred_element_type=jnp.float32
    )
    grad_b = grad_b + jnp.einsum(
        "abts,abtn->absn", grad_scores, c_low, preferred_element_type=jnp.float32
    )
    grad_log = jnp.flip(jnp.cumsum(jnp.flip(grad_cum, 2), axis=2), 2)
    grad_step = grad_step + grad_log * decay_rate
    grad_decay_log = jnp.sum(grad_log * step_blocks, axis=(0, 1, 2)) * decay_rate
    grad_arg = grad_step.reshape(pack_count, local_rows, H) * jax.nn.sigmoid(step_arg)
    grad_step_bias = jnp.sum(grad_arg, axis=(0, 1))
    grad_act = jnp.concatenate(
        [
            grad_x.reshape(pack_count, local_rows, E),
            grad_b.reshape(pack_count, local_rows, N),
            grad_c.reshape(pack_count, local_rows, N),
        ],
        axis=-1,
    )
    grad_pre = grad_act * silu_slope(conv_pre)
    grad_conv_bias = jnp.sum(grad_pre, axis=(0, 1))
    grad_taps = jnp.stack(
        [
            jnp.sum(
                grad_pre * extended[:, tap_index : tap_index + local_rows] * tap_keep[tap_index],
                axis=(0, 1),
            )
            for tap_index in range(KW)
        ]
    )
    grad_ext = jnp.zeros((pack_count, local_rows + edge_rows, CONV), jnp.float32)
    for tap_index in range(KW):
        grad_ext = grad_ext + jnp.pad(
            grad_pre * conv_taps[tap_index] * tap_keep[tap_index],
            ((0, 0), (tap_index, edge_rows - tap_index), (0, 0)),
        )
    grad_edge = from_behind(grad_ext[:, :edge_rows].astype(jnp.bfloat16), "seq", -1).astype(
        jnp.float32
    )
    grad_conv_in = jnp.concatenate(
        [grad_ext[:, edge_rows:local_rows], grad_ext[:, local_rows:] + grad_edge], axis=1
    )
    grad_projected = jnp.concatenate([grad_gate, grad_conv_in, grad_arg], axis=-1).astype(
        jnp.bfloat16
    )
    grad_w_in = jnp.einsum(
        "atd,atj->dj", normed, grad_projected, preferred_element_type=jnp.float32
    )
    grad_normed = jnp.einsum(
        "atj,dj->atd", grad_projected, w_in_low, preferred_element_type=jnp.float32
    )
    grad_gain_in = jnp.sum(grad_normed * scaled, axis=(0, 1))
    grad_scaled = grad_normed * gain_in
    grad_inputs = inv_rms * (
        grad_scaled - scaled * jnp.mean(grad_scaled * scaled, -1, keepdims=True)
    ) + cotangent.astype(jnp.float32)
    grad_vec = jnp.concatenate(
        [
            grad_gain_in,
            grad_gain_out,
            grad_conv_bias,
            grad_taps.reshape(-1),
            grad_step_bias,
            grad_decay_log,
            grad_skip,
        ]
    )
    summed = lax.psum((grad_w_in, grad_w_out, grad_vec), "seq")
    owner_in, owner_out, owner_vec = (
        lax.psum_scatter(summed[0], "dp", scatter_dimension=1, tiled=True),
        lax.psum_scatter(summed[1], "dp", scatter_dimension=0, tiled=True),
        lax.psum_scatter(summed[2], "dp", scatter_dimension=0, tiled=True),
    )
    moment_in = MOMENTUM * in_moment + owner_in
    moment_out = MOMENTUM * out_moment + owner_out
    squares = lax.psum((jnp.sum(moment_in * moment_in), jnp.sum(moment_out * moment_out)), "dp")
    ortho_in = moment_in / (jnp.sqrt(squares[0]) + 1e-07)
    ortho_out = moment_out / (jnp.sqrt(squares[1]) + 1e-07)
    share_rows = 2 * D // lax.axis_size("dp")
    for sweep_index in range(ITERS):

        def gram_part(row_start, row_count, left_part=ortho_in, right_part=ortho_out):
            stacked = jnp.concatenate(
                [
                    jnp.dot(left_part, left_part.T, precision=PRECISE),
                    jnp.dot(right_part.T, right_part, precision=PRECISE),
                ],
                axis=0,
            )
            return stacked

        gram_share = lax.psum_scatter(
            gram_part(jnp.int32(0), share_rows * lax.axis_size("dp")),
            "dp",
            scatter_dimension=0,
            tiled=True,
        )
        gram_full = lax.all_gather(gram_share, "dp", axis=0, tiled=True)
        gram_in = gram_full[:D]
        gram_out = gram_full[D:]
        poly_in = NS_B * gram_in + NS_C * jnp.dot(gram_in, gram_in, precision=PRECISE)
        poly_out = NS_B * gram_out + NS_C * jnp.dot(gram_out, gram_out, precision=PRECISE)
        ortho_in = NS_A * ortho_in + jnp.dot(poly_in, ortho_in, precision=PRECISE)
        ortho_out = NS_A * ortho_out + jnp.dot(ortho_out, poly_out.T, precision=PRECISE)
    weight_in = (
        in_weight * (1.0 - RATE_MATRIX * WEIGHT_DECAY) - RATE_MATRIX * (IN / D) ** 0.5 * ortho_in
    )
    weight_out = (
        out_weight * (1.0 - RATE_MATRIX * WEIGHT_DECAY) - RATE_MATRIX * (E / D) ** 0.5 * ortho_out
    )
    first = BETA_FIRST * vec_moment1 + (1.0 - BETA_FIRST) * owner_vec
    second = BETA_SECOND * vec_moment2 + (1.0 - BETA_SECOND) * owner_vec * owner_vec
    corrected = (
        first
        / (1.0 - BETA_FIRST**STEP)
        / (jnp.sqrt(second / (1.0 - BETA_SECOND**STEP)) + ADAM_EPSILON)
    )
    vec_new = vectors * (1.0 - RATE_VECTOR * WEIGHT_DECAY) - RATE_VECTOR * corrected
    return (
        result,
        grad_inputs,
        moment_in,
        weight_in,
        moment_out,
        weight_out,
        first,
        second,
        vec_new,
    )


def solution(mesh):
    placed = (
        P("dp", "seq", None),
        P("dp", "seq"),
        P("dp", "seq", None),
        P(None, "dp"),
        P("dp", None),
        P("dp"),
        P(None, "dp"),
        P("dp", None),
        P("dp"),
        P("dp"),
    )
    return jax.shard_map(
        per_device,
        mesh=mesh,
        in_specs=placed,
        out_specs=(
            P("dp", "seq", None),
            P("dp", "seq", None),
            P(None, "dp"),
            P(None, "dp"),
            P("dp", None),
            P("dp", None),
            P("dp"),
            P("dp"),
            P("dp"),
        ),
        check_vma=False,
    )
```

profile of v0, /device:TPU:0, one launch (start us, length us, event | category | flops | bytes accessed | tf_op | source)
XLA Modules:
  0.0 1634.6 jit_solution(3623461341099445927)
XLA Ops:
  13.1 13.3 all-reduce.5
  31.7 21.6 %all-gather.28.cloned.1.call-done = bf16[4,838,768]{2,1,0:T(8,128)(2,1)} async-done(((bf16[1,838,768]{2,1,0:T(8,128)(2,1)}), bf16[4,838,768]{2,1,0:T(8,128)(2,1)}) %all-gather.28.cloned.1.call-update) | async-done | bytes 5148688 | tf_op jit(solution)/shard_map/all_gather | solution.py:98
  70.9 21.3 %copy.405 = f32[2,512,3352]{2,0,1:T(2,128)} copy(f32[2,512,3352]{1,2,0:T(8,128)} %fusion.167) | data formatting | bytes 27459584 | tf_op jit(solution)/shard_map/dot_general | solution.py:114
  122.8 28.4 %fusion.245 = (bf16[2,512,1792]{2,0,1:T(2,128)(2,1)}, f32[2,512,1792]{2,0,1:T(2,128)}, f32[2,512,1792]{2,0,1:T(2,128)}) fusion(f32[1792]{0:T(1024)} %get-tuple-element.364, f32[2,515,1792]{2,0,1:T(2,128)} %maximum_convert_fusion, f32[2,512]{0,1:T(8,128)S(1)} %get-tuple-element.349, f32[1792]{0:T(1024)S(1)} %copy-done.82, ...), kind=kLoop, calls=%fused_computation.321 | loop fusion | flops 29360128 | bytes 47758336 | tf_op jit(solution)/shard_map/convert.21
  158.8 12.4 reshape.370
  197.2 18.6 %all-gather = bf16[16,1,24]{2,1,0:T(2,128)(2,1)S(1)} all-gather(bf16[2,1,24]{2,1,0:T(2,128)(2,1)S(1)} %copy-done.110), channel_id=2, replica_groups=mesh['seq'=8,'dp'=4] {'seq'}, dimensions={0}, use_global_device_ids=true | all-gather | bytes 864 | tf_op jit(solution)/shard_map/all_gather | solution.py:42
  217.3 69.6 %all-gather.12.cloned.1.call-done = bf16[8,2,24,64,128]{4,3,2,1,0:T(8,128)(2,1)} async-done(((bf16[1,2,24,64,128]{4,3,2,1,0:T(8,128)(2,1)}), bf16[8,2,24,64,128]{4,3,2,1,0:T(8,128)(2,1)}) %all-gather.12.cloned.1.call-update) | async-done | bytes 6291472 | tf_op jit(solution)/shard_map/all_gather | solution.py:42
  286.8 12.5 while.30
  326.2 12.2 reshape.371
  349.5 15.7 multiply_reduce_fusion.7
  365.2 24.9 %multiply_reduce_fusion.6 = (f32[1536]{0:T(1024)}, f32[2,512,1536]{2,0,1:T(2,128)}, bf16[2,512,1536]{2,0,1:T(2,128)(2,1)}, bf16[2,512,1536]{2,0,1:T(2,128)(2,1)}) fusion(f32[2,512,1792]{2,0,1:T(2,128)} %get-tuple-element.331, f32[2,512,1536]{2,0,1:T(2,128)S(1)} %get-tuple-element.329, f32[2,512,3352]{2,0,1:T(2,128)} %copy.405, ...), kind=kLoop, calls=%fused_computation.37 | loop fusion | flops 28310016 | bytes 50352128 | tf_op jit(solution)/shard_map/reduce_sum | solution.py:215
  426.6 21.3 %fusion.5 = (f32[2,2,24,256]{3,2,1,0:T(8,128)}, f32[2,2,24,256]{3,2,1,0:T(8,128)}, f32[2,2,24,256]{3,2,1,0:T(8,128)}, bf16[2,2,256,256]{3,2,1,0:T(8,128)(2,1)S(1)}) fusion(f32[2,2,24,256]{3,2,1,0:T(8,128)S(1)} %copy-done.70, f32[2,2,24,256]{3,2,1,0:T(8,128)S(1)} %copy-done.76, f32[2,2,256,256]{3,2,1,0:T(8,128)S(1)} %copy-done.57, ...), kind=kOutput, calls=%fused_computation.12 | convolution fusion | flops 888332288 | bytes 11763712 | tf_op jit(solution)/shard_map/abthp,abshp->abhts/dot_general | solution.py:217
  469.6 43.3 %all-gather.16.cloned.1.call-done = bf16[8,2,24,64,128]{4,3,2,1,0:T(8,128)(2,1)} async-done(((bf16[1,2,24,64,128]{4,3,2,1,0:T(8,128)(2,1)}), bf16[8,2,24,64,128]{4,3,2,1,0:T(8,128)(2,1)}) %all-gather.16.cloned.1.call-update) | async-done | bytes 6291472 | tf_op jit(solution)/shard_map/all_gather | solution.py:42
  512.9 13.4 while.31
  557.1 12.4 reshape.367
  570.6 33.9 %multiply_reduce_fusion.5 = (f32[1792]{0:T(1024)S(1)}, f32[1792]{0:T(1024)S(1)}, f32[1792]{0:T(1024)S(1)}, f32[1792]{0:T(1024)S(1)}, f32[1792]{0:T(1024)S(1)}, /*index=5*/f32[2,512,1792]{2,0,1:T(2,128)S(1)}) fusion(f32[2,515,1792]{2,0,1:T(2,128)} %maximum_convert_fusion, f32[2,512]{0,1:T(8,128)S(1)} %copy-done.29, f32[2,512]{0,1:T(8,128)S(1)} %copy-done.33, ...), kind=kLoop, calls=%fused_computation.24 | loop fusion | flops 40361216 | bytes 51428352 | tf_op jit(solution)/shard_map/reduce_sum | solution.py:296
  642.9 31.0 %pad_maximum_fusion = bf16[2,512,3352]{2,0,1:T(2,128)(2,1)} fusion(bf16[2,512,24]{2,0,1:T(2,128)(2,1)S(1)} %get-tuple-element.319, bf16[2,3,1792]{2,0,1:T(2,128)(2,1)S(1)} %fusion.211, bf16[2,509,1792]{2,0,1:T(2,128)(2,1)S(1)} %slice.285, bf16[2,512,1536]{2,0,1:T(2,128)(2,1)S(1)} %copy-done.15), kind=kLoop, calls=%fused_computation.30 | loop fusion | flops 27459584 | bytes 13729792 | tf_op jit(solution)/shard_map/concatenate | solution.py:315
  673.9 18.0 %copy.461 = bf16[2,512,3352]{1,2,0:T(8,128)(2,1)} copy(bf16[2,512,3352]{2,0,1:T(2,128)(2,1)} %pad_maximum_fusion) | data formatting | bytes 13729792 | tf_op jit(solution)/shard_map/concatenate | solution.py:315
  691.9 13.0 convolution_bitcast_fusion
  704.9 90.7 %fusion = f32[768,840]{0,1:T(8,128)S(1)} fusion(f32[768,3352]{0,1:T(8,128)} %convolution_bitcast_fusion), kind=kCustom, calls=%all-reduce-scatter | all-reduce-scatter fusion | flops 2580481 | bytes 12878336
  822.0 135.8 %all-reduce.13.cloned.1.call-done = (f32[768,838]{0,1:T(8,128)}, f32[384,768]{1,0:T(8,128)}) async-done(((f32[768,838]{0,1:T(8,128)}, f32[384,768]{1,0:T(8,128)}), (f32[768,838]{0,1:T(8,128)}, f32[384,768]{1,0:T(8,128)})) %all-reduce.13.cloned.1.call-update) | async-done | bytes 3754000 | tf_op jit(solution)/shard_map/psum | solution.py:340
  963.9 12.9 all-reduce.10
  993.8 46.0 %reduce-scatter.9.cloned.1.call-done = f32[384,768]{1,0:T(8,128)} async-done(((f32[1536,768]{1,0:T(8,128)}), f32[384,768]{1,0:T(8,128)}) %reduce-scatter.9.cloned.1.call-update) | async-done | bytes 1179664 | tf_op jit(solution)/shard_map/reduce_scatter | solution.py:364
  1039.9 39.0 %all-gather.18.cloned.1.call-done = f32[1536,768]{1,0:T(8,128)} async-done(((f32[384,768]{1,0:T(8,128)}), f32[1536,768]{1,0:T(8,128)}) %all-gather.18.cloned.1.call-update) | async-done | bytes 4718608 | tf_op jit(solution)/shard_map/all_gather | solution.py:370
  1120.2 48.0 %reduce-scatter.11.cloned.1.call-done = f32[384,768]{1,0:T(8,128)} async-done(((f32[1536,768]{1,0:T(8,128)}), f32[384,768]{1,0:T(8,128)}) %reduce-scatter.11.cloned.1.call-update) | async-done | bytes 1179664 | tf_op jit(solution)/shard_map/reduce_scatter | solution.py:364
  1168.6 38.5 %all-gather.20.cloned.1.call-done = f32[1536,768]{1,0:T(8,128)} async-done(((f32[384,768]{1,0:T(8,128)}), f32[1536,768]{1,0:T(8,128)}) %all-gather.20.cloned.1.call-update) | async-done | bytes 4718608 | tf_op jit(solution)/shard_map/all_gather | solution.py:370
  1247.1 47.9 %reduce-scatter.13.cloned.1.call-done = f32[384,768]{1,0:T(8,128)} async-done(((f32[1536,768]{1,0:T(8,128)}), f32[384,768]{1,0:T(8,128)}) %reduce-scatter.13.cloned.1.call-update) | async-done | bytes 1179664 | tf_op jit(solution)/shard_map/reduce_scatter | solution.py:364
  1295.5 38.4 %all-gather.22.cloned.1.call-done = f32[1536,768]{1,0:T(8,128)} async-done(((f32[384,768]{1,0:T(8,128)}), f32[1536,768]{1,0:T(8,128)}) %all-gather.22.cloned.1.call-update) | async-done | bytes 4718608 | tf_op jit(solution)/shard_map/all_gather | solution.py:370
  1377.2 47.9 %reduce-scatter.15.cloned.1.call-done = f32[384,768]{1,0:T(8,128)} async-done(((f32[1536,768]{1,0:T(8,128)}), f32[384,768]{1,0:T(8,128)}) %reduce-scatter.15.cloned.1.call-update) | async-done | bytes 1179664 | tf_op jit(solution)/shard_map/reduce_scatter | solution.py:364
  1425.6 38.5 %all-gather.24.cloned.1.call-done = f32[1536,768]{1,0:T(8,128)} async-done(((f32[384,768]{1,0:T(8,128)}), f32[1536,768]{1,0:T(8,128)}) %all-gather.24.cloned.1.call-update) | async-done | bytes 4718608 | tf_op jit(solution)/shard_map/all_gather | solution.py:370
  1504.1 47.9 %reduce-scatter.17.cloned.1.call-done = f32[384,768]{1,0:T(8,128)} async-done(((f32[1536,768]{1,0:T(8,128)}), f32[384,768]{1,0:T(8,128)}) %reduce-scatter.17.cloned.1.call-update) | async-done | bytes 1179664 | tf_op jit(solution)/shard_map/reduce_scatter | solution.py:364
  1562.4 37.5 %psum.42 = f32[2834]{0:T(1024)S(1)} all-reduce(f32[2834]{0:T(1024)S(1)} %dynamic-slice.4), channel_id=1, replica_groups=mesh['seq'=8,'dp'=4] {'seq'}, use_global_device_ids=true, to_apply=%region_49.50 | all-reduce | flops 2834 | bytes 22672 | tf_op jit(solution)/shard_map/psum | solution.py:340
  (500 shorter events, 534.7 us)
Async XLA Ops:
  7.2 46.0 %all-gather.28.cloned.1.call-start = ((), (), s32[]{:S(2)}) async-start(), calls=%async_computation.20 | async-start | bytes 6451200 | tf_op jit(solution)/shard_map/all_gather | solution.py:98
  10.4 179.2 %all-gather.14.cloned.1.call-start = ((), (), s32[]{:S(2)}) async-start(), calls=%async_computation.7 | async-start | bytes 2949120 | tf_op jit(solution)/shard_map/all_gather | solution.py:99
  11.3 275.5 %all-gather.12.cloned.1.call-start = ((), (), s32[]{:S(2)}) async-start(), calls=%async_computation.6 | async-start | bytes 7077888 | tf_op jit(solution)/shard_map/all_gather | solution.py:42
  27.0 73.5 %copy-start.107 = (f32[24]{0:T(128)}, f32[24]{0:T(128)S(1)}, u32[]{:S(2)}) copy-start(f32[24]{0:T(128)S(1)} %get-tuple-element.359) | copy-start | bytes 292
  27.6 95.1 %copy-start.78 = (f32[1792]{0:T(1024)}, f32[1792]{0:T(1024)S(1)}, u32[]{:S(2)}) copy-start(f32[1792]{0:T(1024)S(1)} %get-tuple-element.361) | copy-start | bytes 21508
  27.6 95.1 %copy-start.80 = (f32[1792]{0:T(1024)}, f32[1792]{0:T(1024)S(1)}, u32[]{:S(2)}) copy-start(f32[1792]{0:T(1024)S(1)} %get-tuple-element.362) | copy-start | bytes 21508
  28.2 72.4 %copy-start.111 = (f32[24]{0:T(128)}, f32[24]{0:T(128)S(1)}, u32[]{:S(2)}) copy-start(f32[24]{0:T(128)S(1)} %fusion.214) | copy-start | bytes 292
  30.2 81.5 %copy-start.105 = (f32[2,2]{1,0:T(2,128)}, f32[2,2]{1,0:T(2,128)S(1)}, u32[]{:S(2)}) copy-start(f32[2,2]{1,0:T(2,128)S(1)} %fusion.213) | copy-start | bytes 52
  30.3 81.6 %copy-start.88 = (f32[2,2,256]{2,1,0:T(2,128)}, f32[2,2,256]{2,1,0:T(2,128)S(1)}, u32[]{:S(2)}) copy-start(f32[2,2,256]{2,1,0:T(2,128)S(1)} %get-tuple-element.366) | copy-start | bytes 12292
  30.3 81.6 %copy-start.90 = (f32[2,2,256]{2,1,0:T(2,128)}, f32[2,2,256]{2,1,0:T(2,128)S(1)}, u32[]{:S(2)}) copy-start(f32[2,2,256]{2,1,0:T(2,128)S(1)} %get-tuple-element.365) | copy-start | bytes 12292
  31.7 91.0 %copy-start.28 = (f32[2,512]{0,1:T(8,128)}, f32[2,512]{0,1:T(8,128)S(1)}, u32[]{:S(2)}) copy-start(f32[2,512]{0,1:T(8,128)S(1)} %get-tuple-element.347) | copy-start | bytes 12292
  31.7 91.0 %copy-start.30 = (f32[2,512]{0,1:T(8,128)}, f32[2,512]{0,1:T(8,128)S(1)}, u32[]{:S(2)}) copy-start(f32[2,512]{0,1:T(8,128)S(1)} %get-tuple-element.348) | copy-start | bytes 12292
  31.7 91.0 %copy-start.32 = (f32[2,512]{0,1:T(8,128)}, f32[2,512]{0,1:T(8,128)S(1)}, u32[]{:S(2)}) copy-start(f32[2,512]{0,1:T(8,128)S(1)} %get-tuple-element.349) | copy-start | bytes 12292
  107.4 5.8 collective-permute-start
  182.3 226.7 %copy-start.17 = (bf16[2,512,128]{2,0,1:T(2,128)(2,1)}, bf16[2,512,128]{2,0,1:T(2,128)(2,1)S(1)}, u32[]{:S(2)}) copy-start(bf16[2,512,128]{2,0,1:T(2,128)(2,1)S(1)} %get-tuple-element.342) | copy-start | bytes 786436
  189.0 323.9 %all-gather.16.cloned.1.call-start = ((), (), s32[]{:S(2)}) async-start(), calls=%async_computation.8 | async-start | bytes 7077888 | tf_op jit(solution)/shard_map/all_gather | solution.py:42
  189.6 113.0 %copy-start.64 = (pred[2,2,256,256]{3,2,1,0:T(8,128)(4,1)}, pred[2,2,256,256]{3,2,1,0:T(8,128)(4,1)S(1)}, u32[]{:S(2)}) copy-start(pred[2,2,256,256]{3,2,1,0:T(8,128)(4,1)S(1)} %compare_and_fusion) | copy-start | bytes 786436
  216.0 86.6 %copy-start.69 = (f32[2,2,24,256]{3,2,1,0:T(8,128)}, f32[2,2,24,256]{3,2,1,0:T(8,128)S(1)}, u32[]{:S(2)}) copy-start(f32[2,2,24,256]{3,2,1,0:T(8,128)S(1)} %copy.418) | copy-start | bytes 294916
  415.5 392.9 %reduce-scatter.19.cloned.1.call-start = ((), (), s32[]{:S(2)}) async-start(), calls=%async_computation.19 | async-start | bytes 5898240 | tf_op jit(solution)/shard_map/reduce_scatter | solution.py:343
  469.6 488.3 %all-reduce.13.cloned.1.call-start = ((), (), s32[]{:S(2)}) async-start(), calls=%async_computation.21 | async-start | bytes 7520256 | tf_op jit(solution)/shard_map/psum | solution.py:340
  629.7 12.4 collective-permute-start.1
  795.6 2.1 collective-permute-start.2
  808.5 231.3 %reduce-scatter.9.cloned.1.call-start = ((), (), s32[]{:S(2)}) async-start(), calls=%async_computation.9 | async-start | bytes 5898240 | tf_op jit(solution)/shard_map/reduce_scatter | solution.py:364
  993.7 85.1 %all-gather.18.cloned.1.call-start = ((), (), s32[]{:S(2)}) async-start(), calls=%async_computation.10 | async-start | bytes 5898240 | tf_op jit(solution)/shard_map/all_gather | solution.py:370
  1039.8 128.3 %reduce-scatter.11.cloned.1.call-start = ((), (), s32[]{:S(2)}) async-start(), calls=%async_computation.11 | async-start | bytes 5898240 | tf_op jit(solution)/shard_map/reduce_scatter | solution.py:364
  1120.2 87.0 %all-gather.20.cloned.1.call-start = ((), (), s32[]{:S(2)}) async-start(), calls=%async_computation.12 | async-start | bytes 5898240 | tf_op jit(solution)/shard_map/all_gather | solution.py:370
  1168.2 126.8 %reduce-scatter.13.cloned.1.call-start = ((), (), s32[]{:S(2)}) async-start(), calls=%async_computation.13 | async-start | bytes 5898240 | tf_op jit(solution)/shard_map/reduce_scatter | solution.py:364
  1247.0 86.9 %all-gather.22.cloned.1.call-start = ((), (), s32[]{:S(2)}) async-start(), calls=%async_computation.14 | async-start | bytes 5898240 | tf_op jit(solution)/shard_map/all_gather | solution.py:370
  1295.0 130.1 %reduce-scatter.15.cloned.1.call-start = ((), (), s32[]{:S(2)}) async-start(), calls=%async_computation.15 | async-start | bytes 5898240 | tf_op jit(solution)/shard_map/reduce_scatter | solution.py:364
  1377.1 87.0 %all-gather.24.cloned.1.call-start = ((), (), s32[]{:S(2)}) async-start(), calls=%async_computation.16 | async-start | bytes 5898240 | tf_op jit(solution)/shard_map/all_gather | solution.py:370
  1425.1 126.9 %reduce-scatter.17.cloned.1.call-start = ((), (), s32[]{:S(2)}) async-start(), calls=%async_computation.17 | async-start | bytes 5898240 | tf_op jit(solution)/shard_map/reduce_scatter | solution.py:364
  1504.0 96.5 %all-gather.26.cloned.1.call-start = ((), (), s32[]{:S(2)}) async-start(), calls=%async_computation.18 | async-start | bytes 5898240 | tf_op jit(solution)/shard_map/all_gather | solution.py:370
  (115 other events, 1318.6 us)
Sparse Core Ops, SparseCore 0:
  10.5 42.7 all-gather.27
  55.4 24.1 all-gather.13
  189.1 97.6 all-gather.11
  415.7 97.1 all-gather.15
  515.3 46.0 reduce-scatter.18
  808.6 149.2 all-reduce.12
  993.9 45.8 reduce-scatter.8
  1041.4 37.4 all-gather.17
  1120.3 47.8 reduce-scatter.10
  1169.6 37.4 all-gather.19
  1247.2 47.8 reduce-scatter.12
  1296.4 37.4 all-gather.21
  1377.3 47.8 reduce-scatter.14
  1426.6 37.4 all-gather.23
  1504.2 47.8 reduce-scatter.16
  1553.5 37.4 all-gather.25
where the time goes:
time: 1650 us; the launch traced here: 1630 us
  waiting for transfers between devices  663 us (40%)
  matrix products  305 us (18%)
  other arithmetic  272 us (16%)
  local copies, waits for them, and re-layouts  193 us (12%)
  blocking collectives  173 us (10%)
  between operations  19.3 us (1%)
    reduce_scatter x5, waiting for transfers between devices, per_device(): lax.psum_scatter(gram_part(jnp.int32(0), share_rows * lax.axis_size('dp')...  238 us
    all_gather x5, waiting for transfers between devices, per_device(): gram_full = lax.all_gather(gram_share, 'dp', axis=0, tiled=True)  154 us
    psum x1, waiting for transfers between devices, per_device(): summed = lax.psum((grad_w_in, grad_w_out, grad_vec), 'seq')  136 us
    all_gather x2, waiting for transfers between devices, prefix(): lax.all_gather(part.astype(kind), axis)  113 us
    unnamed x2, blocking collectives  104 us
    another operation x16, other arithmetic  57.7 us
    dot_general x5, matrix products, gram_part(): jnp.dot(left_part, left_part.T, precision=PRECISE)  42.8 us
    dot_general x5, matrix products, per_device(): jnp.dot(gram_out, gram_out, precision=PRECISE)  42.6 us
  transfers between devices with their start and end apart: 19, of which 14 were waited for; matrix products, arithmetic and copies ran while one was open for 31% of the time, Pallas kernels for 0%

commit v1 on v0

--- a/solution.py
+++ b/solution.py
@@ -36,24 +36,39 @@
     return lax.ppermute(x, axis, pairs)
 
 
-def prefix(x, axis, combine, identity, reverse):
-    devices, here = (lax.axis_size(axis), lax.axis_index(axis))
-    everything = jax.tree.map(
-        lambda part, kind: lax.all_gather(part.astype(kind), axis), x, (jnp.bfloat16, jnp.bfloat16)
-    )
-    start = jax.tree.map(
-        lambda part, zero: jnp.broadcast_to(jnp.asarray(zero, part.dtype), part.shape), x, identity
-    )
-
-    def hop(k, before):
+def prefix(decay, state, axis, reverse):
+    devices = lax.axis_size(axis)
+    packs, heads, rows, cols = state.shape
+    width = rows // devices * cols
+    parts = state.reshape(packs * heads, devices, width)
+    scales = jnp.broadcast_to(decay.reshape(packs * heads, 1, 1), (packs * heads, devices, cols))
+    sent = jnp.moveaxis(jnp.concatenate([parts, scales], axis=2).astype(jnp.bfloat16), 1, 0)
+    got = lax.all_to_all(sent, axis, 0, 0, tiled=True).astype(jnp.float32)
+    before = jnp.zeros((packs * heads, width), jnp.float32)
+    entering = [None] * devices
+    for k in range(devices):
         at = devices - 1 - k if reverse else k
-        reached = at > here if reverse else at < here
-        new = combine(
-            before, jax.tree.map(lambda part, own: part[at].astype(own.dtype), everything, x)
-        )
-        return jax.tree.map(lambda a, b: jnp.where(reached, a, b), new, before)
-
-    return lax.fori_loop(0, devices, hop, start)
+        entering[at] = before.astype(jnp.bfloat16)
+        before = got[at, :, width : width + 1] * before + got[at, :, :width]
+    back = lax.all_to_all(jnp.stack(entering), axis, 0, 0, tiled=True)
+    return jnp.moveaxis(back, 0, 1).reshape(state.shape).astype(jnp.float32)
+
+
+def orthogonal_factor(gram):
+    size = gram.shape[0]
+    eye = jnp.eye(size, dtype=jnp.float32)
+    norm = jnp.sqrt(jnp.sum(gram * eye)) + 1e-07
+    inverse = 1.0 / norm
+    gram = gram * inverse * inverse
+    factor = None
+    for sweep_index in range(ITERS):
+        precision = PRECISE if sweep_index < 2 else lax.Precision.HIGH
+        square = jnp.dot(gram, gram, precision=precision)
+        poly = NS_A * eye + NS_B * gram + NS_C * square
+        factor = poly if factor is None else jnp.dot(poly, factor, precision=precision)
+        if sweep_index < ITERS - 1:
+            gram = jnp.dot(jnp.dot(poly, gram, precision=precision), poly, precision=precision)
+    return factor * inverse
 
 
 def split_vector(packed):
@@ -72,14 +87,6 @@
 def silu_slope(value):
     sigma = jax.nn.sigmoid(value)
     return sigma * (1.0 + value * (1.0 - sigma))
-
-
-def combine_forward(earlier, later):
-    return (earlier[0] * later[0], later[0][..., None, None] * earlier[1] + later[1])
-
-
-def combine_backward(earlier, later):
-    return (later[0] * earlier[0], later[1] + later[0][..., None, None] * earlier[1])
 
 
 def per_device(
@@ -174,13 +181,7 @@
         block_decay[:, block_index][..., None, None] * state_total + block_state[:, block_index]
     )
     decay_total = decay_total * block_decay[:, block_index]
-    entering = prefix(
-        (decay_total, state_total),
-        "seq",
-        combine_forward,
-        (jnp.ones_like(decay_total), jnp.zeros_like(state_total)),
-        False,
-    )[1]
+    entering = prefix(decay_total, state_total, "seq", False)
     state_list = [entering]
     block_index = 0
     state_list.append(
@@ -231,13 +232,7 @@
     local_adjoint = (
         grad_state_in[:, block_index] + block_decay[:, block_index][..., None, None] * local_adjoint
     )
-    adjoint_next = prefix(
-        (decay_total, local_adjoint),
-        "seq",
-        combine_backward,
-        (jnp.ones_like(decay_total), jnp.zeros_like(local_adjoint)),
-        True,
-    )[1]
+    adjoint_next = prefix(decay_total, local_adjoint, "seq", True)
     state_grads = [None] * block_count
     decay_grads = [None] * block_count
     for block_index in range(block_count - 1, -1, -1):
@@ -315,9 +310,21 @@
     grad_projected = jnp.concatenate([grad_gate, grad_conv_in, grad_arg], axis=-1).astype(
         jnp.bfloat16
     )
+    owners = lax.axis_size("dp")
+    owner_out = lax.psum(
+        lax.psum_scatter(grad_w_out, "dp", scatter_dimension=0, tiled=True), "seq"
+    )
+    grad_projected, owner_out = lax.optimization_barrier((grad_projected, owner_out))
     grad_w_in = jnp.einsum(
-        "atd,atj->dj", normed, grad_projected, preferred_element_type=jnp.float32
-    )
+        "atj,atd->jd", grad_projected, normed, preferred_element_type=jnp.float32
+    ).astype(jnp.bfloat16)
+    owner_in = lax.psum(
+        lax.psum_scatter(
+            grad_w_in.reshape(owners, IN // owners, D), "dp", scatter_dimension=0, tiled=False
+        ),
+        "seq",
+    )
+    owner_in = owner_in.astype(jnp.float32).T
     grad_normed = jnp.einsum(
         "atj,dj->atd", grad_projected, w_in_low, preferred_element_type=jnp.float32
     )
@@ -337,43 +344,19 @@
             grad_skip,
         ]
     )
-    summed = lax.psum((grad_w_in, grad_w_out, grad_vec), "seq")
-    owner_in, owner_out, owner_vec = (
-        lax.psum_scatter(summed[0], "dp", scatter_dimension=1, tiled=True),
-        lax.psum_scatter(summed[1], "dp", scatter_dimension=0, tiled=True),
-        lax.psum_scatter(summed[2], "dp", scatter_dimension=0, tiled=True),
-    )
+    summed_vec = lax.psum(grad_vec, ("seq", "dp"))
+    vec_rows = vectors.shape[0]
+    owner_vec = lax.dynamic_slice(summed_vec, (lax.axis_index("dp") * vec_rows,), (vec_rows,))
+    moment_out = MOMENTUM * out_moment + owner_out
+    gram_out = lax.psum(jnp.dot(moment_out.T, moment_out, precision=PRECISE), "dp")
     moment_in = MOMENTUM * in_moment + owner_in
-    moment_out = MOMENTUM * out_moment + owner_out
-    squares = lax.psum((jnp.sum(moment_in * moment_in), jnp.sum(moment_out * moment_out)), "dp")
-    ortho_in = moment_in / (jnp.sqrt(squares[0]) + 1e-07)
-    ortho_out = moment_out / (jnp.sqrt(squares[1]) + 1e-07)
-    share_rows = 2 * D // lax.axis_size("dp")
-    for sweep_index in range(ITERS):
-
-        def gram_part(row_start, row_count, left_part=ortho_in, right_part=ortho_out):
-            stacked = jnp.concatenate(
-                [
-                    jnp.dot(left_part, left_part.T, precision=PRECISE),
-                    jnp.dot(right_part.T, right_part, precision=PRECISE),
-                ],
-                axis=0,
-            )
-            return stacked
-
-        gram_share = lax.psum_scatter(
-            gram_part(jnp.int32(0), share_rows * lax.axis_size("dp")),
-            "dp",
-            scatter_dimension=0,
-            tiled=True,
-        )
-        gram_full = lax.all_gather(gram_share, "dp", axis=0, tiled=True)
-        gram_in = gram_full[:D]
-        gram_out = gram_full[D:]
-        poly_in = NS_B * gram_in + NS_C * jnp.dot(gram_in, gram_in, precision=PRECISE)
-        poly_out = NS_B * gram_out + NS_C * jnp.dot(gram_out, gram_out, precision=PRECISE)
-        ortho_in = NS_A * ortho_in + jnp.dot(poly_in, ortho_in, precision=PRECISE)
-        ortho_out = NS_A * ortho_out + jnp.dot(ortho_out, poly_out.T, precision=PRECISE)
+    gram_in = jnp.dot(moment_in, moment_in.T, precision=PRECISE)
+    gram_in, gram_out = lax.optimization_barrier((gram_in, gram_out))
+    gram_in = lax.psum(gram_in, "dp")
+    factor_out = orthogonal_factor(gram_out)
+    ortho_out = jnp.dot(moment_out, factor_out.T, precision=lax.Precision.HIGH)
+    factor_in = orthogonal_factor(gram_in)
+    ortho_in = jnp.dot(factor_in, moment_in, precision=lax.Precision.HIGH)
     weight_in = (
         in_weight * (1.0 - RATE_MATRIX * WEIGHT_DECAY) - RATE_MATRIX * (IN / D) ** 0.5 * ortho_in
     )

time: 1650 us -> 1110 us (0.67)
  waiting for transfers between devices: 663 us -> 230 us
  blocking collectives: 173 us -> 53 us
  other arithmetic: 272 us -> 252 us
  local copies, waits for them, and re-layouts: 193 us -> 211 us
    all_gather x7 -> x0, waiting for transfers between devices: 267 us -> none  [the longest x5 154 us: per_device(): gram_full = lax.all_gather(gram_share, 'dp', axis=0, tiled=True)]
    reduce_scatter x6 -> x2, waiting for transfers between devices: 238 us -> 42.1 us  [the longest x1 42.1 us: per_device(): lax.psum_scatter(grad_w_in.reshape(owners, IN // owners, D), 'dp', scatte...]
    unnamed x2 -> x1, blocking collectives: 104 us -> 12.9 us
    all_to_all x0 -> x4, waiting for transfers between devices: none -> 36.3 us  [the longest x2 21.4 us: prefix(): got = lax.all_to_all(sent, axis, 0, 0, tiled=True).astype(jnp.float32)]
    select_n x16 -> x0, other arithmetic: 25.1 us -> none  [hop(): return jax.tree.map(lambda a, b: jnp.where(reached, a, b), new, before)]
    all_to_all x0 -> x4, starting transfers between devices: none -> 18.8 us  [the longest x2 9.78 us: prefix(): back = lax.all_to_all(jnp.stack(entering), axis, 0, 0, tiled=True)]
    all_gather x1 -> x0, blocking collectives: 18.6 us -> none  [prefix(): lax.all_gather(part.astype(kind), axis)]
    optimization_barrier x0 -> x1, local copies, waits for them, and re-layouts: none -> 17.9 us  [per_device(): lax.optimization_barrier((grad_projected, owner_out))]
  transfers between devices with their start and end apart: 19 -> 14, of which waited for: 14 -> 9; matrix products, arithmetic and copies ran while one was open for 31% -> 31% of each run, Pallas kernels for 0% -> 0%
where the time goes in v1:
time: 1110 us; the launch traced here: 1100 us
  matrix products  308 us (28%)
  other arithmetic  252 us (23%)
  waiting for transfers between devices  230 us (21%)
  local copies, waits for them, and re-layouts  211 us (19%)
  blocking collectives  53 us (5%)
  starting transfers between devices  24 us (2%)
  between operations  18.4 us (2%)
    another operation x21, other arithmetic  57.2 us
    psum x1, waiting for transfers between devices, per_device(): lax.psum(lax.psum_scatter(grad_w_out, 'dp', scatter_dimension=0, tiled=Tr...  50.6 us
    dot_general x10, matrix products, orthogonal_factor(): square = jnp.dot(gram, gram, precision=precision)  44.7 us
    psum x1, waiting for transfers between devices, per_device(): lax.psum(jnp.dot(moment_out.T, moment_out, precision=PRECISE), 'dp')  44 us
    reduce_scatter x1, waiting for transfers between devices, per_device(): lax.psum_scatter(grad_w_in.reshape(owners, IN // owners, D), 'dp', scatte...  42.1 us
    dot_general x8, matrix products, orthogonal_factor(): jnp.dot(jnp.dot(poly, gram, precision=precision), poly, precision=precision)  41 us
    psum x1, blocking collectives, per_device(): summed_vec = lax.psum(grad_vec, ('seq', 'dp'))  40.1 us
    dot_general x8, matrix products, orthogonal_factor(): jnp.dot(poly, gram, precision=precision)  39.7 us
  transfers between devices with their start and end apart: 14, of which 9 were waited for; matrix products, arithmetic and copies ran while one was open for 31% of the time, Pallas kernels for 0%

profile of v1, /device:TPU:0, one launch (start us, length us, event | category | flops | bytes accessed | tf_op | source)
XLA Modules:
  0.0 1096.4 jit_solution(15707389335084350312)
XLA Ops:
  11.9 12.9 %all-reduce.5 = bf16[11336]{0:T(1024)(128)(2,1)S(1)} all-reduce(bf16[11336]{0:T(1024)(128)(2,1)S(1)} %dynamic-update-slice), channel_id=1, replica_groups=mesh['seq'=8,'dp'=4] {'dp'}, use_global_device_ids=true, to_apply=%add.5 | all-reduce | flops 11336 | bytes 45344
  29.1 24.1 %all-gather.6.cloned.1.call-done = bf16[4,838,768]{2,1,0:T(8,128)(2,1)} async-done(((bf16[1,838,768]{2,1,0:T(8,128)(2,1)}), bf16[4,838,768]{2,1,0:T(8,128)(2,1)}) %all-gather.6.cloned.1.call-update) | async-done | bytes 5148688 | tf_op jit(solution)/shard_map/all_gather | solution.py:105
  59.2 11.4 %fusion.129 = f32[2,512,3352]{1,2,0:T(8,128)} fusion(bf16[3352,768,1]{1,0,2:T(8,128)(2,1)} %reshape.698, bf16[2,512,768]{2,1,0:T(8,128)(2,1)S(1)} %copy-done.28, f32[768]{0:T(1024)S(1)} %slice.324, f32[2,512]{1,0:T(2,128)S(1)} %add_rsqrt_fusion.1), kind=kOutput, calls=%fused_computation.154 | convolution fusion | flops 5275385856 | bytes 20458496 | tf_op jit(solution)/shard_map/dot_general | solution.py:121
  70.6 21.3 %copy.466 = f32[2,512,3352]{2,0,1:T(2,128)} copy(f32[2,512,3352]{1,2,0:T(8,128)} %fusion.129) | data formatting | bytes 27459584 | tf_op jit(solution)/shard_map/dot_general | solution.py:121
  121.6 25.2 %fusion.383 = (bf16[2,512,1792]{2,0,1:T(2,128)(2,1)}, f32[2,512,1792]{2,0,1:T(2,128)}, f32[2,512,1792]{2,0,1:T(2,128)}) fusion(f32[1792]{0:T(1024)S(1)} %get-tuple-element.103, f32[2,515,1792]{2,0,1:T(2,128)} %maximum_convert_fusion, f32[2,512]{0,1:T(8,128)S(1)} %get-tuple-element.88, f32[1792]{0:T(1024)S(1)} %get-tuple-element.102, ...), kind=kLoop, calls=%fused_computation.496 | loop fusion | flops 29360128 | bytes 47758336 | tf_op jit(solution)/shard_map/convert.27
  154.4 12.5 %reshape.710 = f32[2,2,256,24,64]{4,3,0,2,1:T(8,128)} reshape(f32[2,512,1536]{2,0,1:T(2,128)} %slice.336) | data formatting | bytes 12582912 | tf_op jit(solution)/shard_map/reshape | solution.py:150
  166.9 9.8 copy.472
  196.1 21.4 %all-to-all-done = bf16[8,48,1152]{2,1,0:T(8,128)(2,1)S(1)} async-done(((bf16[8,48,1152]{2,1,0:T(8,128)(2,1)}), bf16[8,48,1152]{2,1,0:T(8,128)(2,1)S(1)}, u32[]{:S(2)}, u32[]{:S(2)}) %all-to-all-start) | async-done | bytes 884768 | tf_op jit(solution)/shard_map/all_to_all | solution.py:46
  235.2 11.0 %all-to-all-done.1 = bf16[8,48,1024]{2,1,0:T(8,128)(2,1)S(1)} async-done(((bf16[8,48,1024]{2,1,0:T(8,128)(2,1)}), bf16[8,48,1024]{2,1,0:T(8,128)(2,1)S(1)}, u32[]{:S(2)}, u32[]{:S(2)}) %all-to-all-start.1) | async-done | bytes 786464 | tf_op jit(solution)/shard_map/all_to_all | solution.py:53
  266.3 11.4 %copy.547 = f32[2,2,256,24,64]{4,3,0,2,1:T(8,128)} copy(f32[2,2,256,24,64]{2,4,3,1,0:T(8,128)} %fusion.11) | data formatting | bytes 12582912 | tf_op jit(solution)/shard_map/reshape | solution.py:195
  277.7 12.4 %reshape.711 = f32[2,512,1536]{2,0,1:T(2,128)} reshape(f32[2,2,256,24,64]{4,3,0,2,1:T(8,128)} %copy.547) | data formatting | bytes 12582912 | tf_op jit(solution)/shard_map/reshape | solution.py:195
  290.1 11.3 %multiply_reduce_fusion.10 = (f32[2,512]{0,1:T(8,128)S(1)}, f32[2,512,1536]{2,0,1:T(2,128)S(1)}, f32[2,512,1536]{2,0,1:T(2,128)S(1)}) fusion(f32[2,512,1536]{2,0,1:T(2,128)} %reshape.711, f32[2,512,3352]{2,0,1:T(2,128)} %copy.466), kind=kLoop, calls=%fused_computation.49 | loop fusion | flops 11009024 | bytes 25169920 | tf_op jit(solution)/shard_map/reduce_sum | solution.py:198
  301.5 15.7 %multiply_reduce_fusion.7 = (f32[1536]{0:T(1024)}, f32[2,512]{0,1:T(8,128)S(1)}) fusion(f32[2,512,1536]{2,1,0:T(8,128)} %fusion.51, f32[2,512,1536]{2,0,1:T(2,128)S(1)} %get-tuple-element.61, f32[2,512]{0,1:T(8,128)S(1)} %add_rsqrt_fusion, f32[1536]{0:T(1024)S(1)} %slice.368), kind=kLoop, calls=%fused_computation.42 | loop fusion | flops 9434624 | bytes 12603392 | tf_op jit(solution)/shard_map/reduce_sum | solution.py:205
  317.2 25.4 %multiply_reduce_fusion.6 = (f32[1536]{0:T(1024)}, f32[2,512,1536]{2,0,1:T(2,128)}, bf16[2,512,1536]{2,0,1:T(2,128)(2,1)}, bf16[2,512,1536]{2,0,1:T(2,128)(2,1)}) fusion(f32[2,512,1792]{2,0,1:T(2,128)S(1)} %bitcast.212, f32[2,512,1536]{2,0,1:T(2,128)S(1)} %get-tuple-element.62, f32[2,512,3352]{2,0,1:T(2,128)} %copy.466, ...), kind=kLoop, calls=%fused_computation.41 | loop fusion | flops 28310016 | bytes 50352128 | tf_op jit(solution)/shard_map/reduce_sum | solution.py:216
  342.6 10.2 copy.497
  381.4 20.4 %fusion.2 = (f32[2,2,24,256]{3,2,1,0:T(8,128)}, f32[2,2,24,256]{3,2,1,0:T(8,128)}, f32[2,2,24,256]{3,2,1,0:T(8,128)}, bf16[2,2,256,256]{3,2,1,0:T(8,128)(2,1)}) fusion(f32[2,2,24,256]{3,2,1,0:T(8,128)} %copy.479, f32[2,2,24,256]{3,2,1,0:T(8,128)} %get-tuple-element.93, f32[2,2,256,256]{3,2,1,0:T(8,128)} %fusion.250, ...), kind=kOutput, calls=%fused_computation.6 | convolution fusion | flops 888332288 | bytes 11763712 | tf_op jit(solution)/shard_map/abthp,abshp->abhts/dot_general | solution.py:218
  472.5 16.3 %fusion.10 = f32[2,2,256,24,64]{2,4,3,1,0:T(8,128)} fusion(f32[2,2,256,24,64]{2,4,3,1,0:T(8,128)} %get-tuple-element.109, f32[2,2,256,24,64]{2,1,4,3,0:T(2,128)} %reshape.679, f32[24]{0:T(128)S(1)} %copy-done.107, f32[2,2,256,24]{2,3,1,0:T(8,128)S(1)} %copy-done.50, f32[2,2,24,256]{3,2,1,0:T(8,128)S(1)} %copy-done.68, f32[2,2,24,256]{3,2,1,0:T(8,128)S(1)} %copy-done.70, ...), kind=kOutput, calls=%fused_computation.38 | convolution fusion | flops 843055104 | bytes 23625824 | tf_op jit(solution)/shard_map/abhts,abthp->abshp/dot_general | solution.py:221
  488.8 11.4 %copy.543 = f32[2,2,256,24,64]{4,3,0,2,1:T(8,128)} copy(f32[2,2,256,24,64]{2,4,3,1,0:T(8,128)} %fusion.10) | data formatting | bytes 12582912 | tf_op jit(solution)/shard_map/reshape | solution.py:281
  500.2 12.4 %reshape.709 = f32[2,512,1536]{2,0,1:T(2,128)} reshape(f32[2,2,256,24,64]{4,3,0,2,1:T(8,128)} %copy.543) | data formatting | bytes 12582912 | tf_op jit(solution)/shard_map/reshape | solution.py:281
  512.6 35.2 %multiply_reduce_fusion.5 = (f32[1792]{0:T(1024)}, f32[1792]{0:T(1024)}, f32[1792]{0:T(1024)}, f32[1792]{0:T(1024)}, f32[1792]{0:T(1024)}, /*index=5*/f32[2,512,1792]{2,0,1:T(2,128)}) fusion(f32[2,515,1792]{2,0,1:T(2,128)} %maximum_convert_fusion, f32[2,512]{0,1:T(8,128)S(1)} %copy-done.35, f32[2,512]{0,1:T(8,128)S(1)} %copy-done.40, ...), kind=kLoop, calls=%fused_computation.28 | loop fusion | flops 40361216 | bytes 51428352 | tf_op jit(solution)/shard_map/reduce_sum | solution.py:291
  563.1 12.7 %multiply_multiply_fusion.3 = (f32[2,512,1792]{2,0,1:T(2,128)S(1)}, f32[2,512,1792]{2,0,1:T(2,128)S(1)}, f32[2,512,1792]{2,0,1:T(2,128)S(1)}, f32[2,512,1792]{2,0,1:T(2,128)S(1)}) fusion(f32[2,512,1792]{2,0,1:T(2,128)} %get-tuple-element.53, f32[2,512]{0,1:T(8,128)S(1)} %copy-done.35, f32[1792]{0:T(1024)S(1)} %copy-done.72, f32[1792]{0:T(1024)S(1)} %copy-done.78, ...), kind=kLoop, calls=%fused_computation.31 | loop fusion | flops 12845056 | bytes 36741120 | tf_op jit(solution)/shard_map/mul | solution.py:301
  593.1 29.0 %pad_maximum_fusion = bf16[2,512,3352]{2,0,1:T(2,128)(2,1)} fusion(bf16[2,512,24]{2,0,1:T(2,128)(2,1)S(1)} %get-tuple-element.52, bf16[2,3,1792]{2,0,1:T(2,128)(2,1)S(1)} %fusion.267, bf16[2,509,1792]{2,0,1:T(2,128)(2,1)} %slice.385, bf16[2,512,1536]{2,0,1:T(2,128)(2,1)S(1)} %copy-done.14), kind=kLoop, calls=%fused_computation.34 | loop fusion | flops 27459584 | bytes 13729792 | tf_op jit(solution)/shard_map/concatenate | solution.py:310
  622.0 50.6 %all-reduce.11.cloned.1.call-done = f32[384,768]{1,0:T(8,128)} async-done(((f32[384,768]{1,0:T(8,128)}), f32[384,768]{1,0:T(8,128)}) %all-reduce.11.cloned.1.call-update) | async-done | bytes 1179664 | tf_op jit(solution)/shard_map/psum | solution.py:314
  672.7 17.9 %copy.524 = bf16[2,512,3352]{1,2,0:T(8,128)(2,1)} copy(bf16[2,512,3352]{2,0,1:T(2,128)(2,1)} %pad_maximum_fusion) | data formatting | bytes 13729792 | tf_op jit(solution)/shard_map/optimization_barrier | solution.py:317
  690.6 12.2 %bitcast_convert_fusion = bf16[3352,768]{1,0:T(8,128)(2,1)} fusion(bf16[2,512,3352]{1,2,0:T(8,128)(2,1)} %copy.524, bf16[2,512,768]{2,1,0:T(8,128)(2,1)S(1)} %copy-done.29, f32[768]{0:T(1024)S(1)} %copy-done.94, f32[2,512]{1,0:T(2,128)S(1)} %copy-done.96), kind=kOutput, calls=%fused_computation.10 | convolution fusion | flops 5277960192 | bytes 13593600 | tf_op jit(solution)/shard_map/atj,atd->jd/dot_general | solution.py:318
  717.1 42.1 %reduce-scatter.5.cloned.1.call-done = bf16[1,838,768]{2,1,0:T(8,128)(2,1)} async-done(((bf16[4,838,768]{2,1,0:T(8,128)(2,1)}), bf16[1,838,768]{2,1,0:T(8,128)(2,1)}) %reduce-scatter.5.cloned.1.call-update) | async-done | bytes 1287184 | tf_op jit(solution)/shard_map/reduce_scatter | solution.py:322
  759.3 12.0 %fusion.21 = (f32[768]{0:T(1024)S(1)}, f32[2,512]{1,0:T(2,128)S(1)}, f32[2,512,768]{2,1,0:T(8,128)}) fusion(bf16[2,512,768]{2,1,0:T(8,128)(2,1)S(1)} %copy-done.29, f32[2,512]{1,0:T(2,128)S(1)} %copy-done.96, f32[768]{0:T(1024)S(1)} %copy-done.94, bf16[2,512,3352]{1,2,0:T(8,128)(2,1)} %copy.524, bf16[3352,768,1]{1,0,2:T(8,128)(2,1)} %reshape.698), kind=kOutput, calls=%fused_computation.68 | convolution fusion | flops 5277743104 | bytes 16746496 | tf_op jit(solution)/shard_map/atj,dj->atd/dot_general | solution.py:328
  771.4 40.1 %psum.39 = f32[11336]{0:T(1024)S(1)} all-reduce(f32[11336]{0:T(1024)S(1)} %concatenate.40), channel_id=1, replica_groups=mesh['seq'=8,'dp'=4] {'seq','dp'}, use_global_device_ids=true, to_apply=%region_40.41 | all-reduce | flops 11336 | bytes 90688 | tf_op jit(solution)/shard_map/psum | solution.py:347
  825.0 21.3 %all-reduce.13.cloned.1.call-done = bf16[768,838]{0,1:T(8,128)(2,1)} async-done(((bf16[768,838]{0,1:T(8,128)(2,1)}), bf16[768,838]{0,1:T(8,128)(2,1)}) %all-reduce.13.cloned.1.call-update) | async-done | bytes 1287184 | tf_op jit(solution)/shard_map/psum | solution.py:321
  850.2 9.3 fusion.394
  859.5 44.0 %all-reduce.15.cloned.1.call-done = f32[768,768]{1,0:T(8,128)} async-done(((f32[768,768]{1,0:T(8,128)}), f32[768,768]{1,0:T(8,128)}) %all-reduce.15.cloned.1.call-update) | async-done | bytes 2359312 | tf_op jit(solution)/shard_map/psum | solution.py:351
  992.1 11.1 %all-reduce.17.cloned.1.call-done = f32[768,768]{1,0:T(8,128)} async-done(((f32[768,768]{1,0:T(8,128)}), f32[768,768]{1,0:T(8,128)}) %all-reduce.17.cloned.1.call-update) | async-done | bytes 2359312 | tf_op jit(solution)/shard_map/psum | solution.py:355
  (468 shorter events, 444.2 us)
Async XLA Ops:
  7.2 46.0 %all-gather.6.cloned.1.call-start = ((), (), s32[]{:S(2)}) async-start(), calls=%async_computation.13 | async-start | bytes 6451200 | tf_op jit(solution)/shard_map/all_gather | solution.py:105
  28.6 82.3 %copy-start.100 = (f32[2,2]{1,0:T(2,128)}, f32[2,2]{1,0:T(2,128)S(1)}, u32[]{:S(2)}) copy-start(f32[2,2]{1,0:T(2,128)S(1)} %fusion.271) | copy-start | bytes 52
  28.7 76.1 %copy-start.102 = (f32[24]{0:T(128)}, f32[24]{0:T(128)S(1)}, u32[]{:S(2)}) copy-start(f32[24]{0:T(128)S(1)} %get-tuple-element.98) | copy-start | bytes 292
  28.7 224.3 %copy-start.106 = (f32[24]{0:T(128)}, f32[24]{0:T(128)S(1)}, u32[]{:S(2)}) copy-start(f32[24]{0:T(128)S(1)} %get-tuple-element.97) | copy-start | bytes 292
  28.8 76.0 %copy-start.104 = (f32[24]{0:T(128)}, f32[24]{0:T(128)S(1)}, u32[]{:S(2)}) copy-start(f32[24]{0:T(128)S(1)} %fusion.272) | copy-start | bytes 292
  28.9 83.1 %copy-start.82 = (f32[2,2,256]{2,1,0:T(2,128)}, f32[2,2,256]{2,1,0:T(2,128)S(1)}, u32[]{:S(2)}) copy-start(f32[2,2,256]{2,1,0:T(2,128)S(1)} %get-tuple-element.105) | copy-start | bytes 12292
  28.9 83.1 %copy-start.83 = (f32[2,2,256]{2,1,0:T(2,128)}, f32[2,2,256]{2,1,0:T(2,128)S(1)}, u32[]{:S(2)}) copy-start(f32[2,2,256]{2,1,0:T(2,128)S(1)} %get-tuple-element.104) | copy-start | bytes 12292
  28.9 92.6 %copy-start.71 = (f32[1792]{0:T(1024)}, f32[1792]{0:T(1024)S(1)}, u32[]{:S(2)}) copy-start(f32[1792]{0:T(1024)S(1)} %get-tuple-element.100) | copy-start | bytes 21508
  28.9 92.6 %copy-start.73 = (f32[1792]{0:T(1024)}, f32[1792]{0:T(1024)S(1)}, u32[]{:S(2)}) copy-start(f32[1792]{0:T(1024)S(1)} %get-tuple-element.101) | copy-start | bytes 21508
  28.9 92.6 %copy-start.75 = (f32[1792]{0:T(1024)}, f32[1792]{0:T(1024)S(1)}, u32[]{:S(2)}) copy-start(f32[1792]{0:T(1024)S(1)} %get-tuple-element.102) | copy-start | bytes 21508
  28.9 92.6 %copy-start.77 = (f32[1792]{0:T(1024)}, f32[1792]{0:T(1024)S(1)}, u32[]{:S(2)}) copy-start(f32[1792]{0:T(1024)S(1)} %get-tuple-element.103) | copy-start | bytes 21508
  29.1 92.5 %copy-start.34 = (f32[2,512]{0,1:T(8,128)}, f32[2,512]{0,1:T(8,128)S(1)}, u32[]{:S(2)}) copy-start(f32[2,512]{0,1:T(8,128)S(1)} %get-tuple-element.86) | copy-start | bytes 12292
  29.1 92.5 %copy-start.36 = (f32[2,512]{0,1:T(8,128)}, f32[2,512]{0,1:T(8,128)S(1)}, u32[]{:S(2)}) copy-start(f32[2,512]{0,1:T(8,128)S(1)} %get-tuple-element.87) | copy-start | bytes 12292
  29.1 92.5 %copy-start.39 = (f32[2,512]{0,1:T(8,128)}, f32[2,512]{0,1:T(8,128)S(1)}, u32[]{:S(2)}) copy-start(f32[2,512]{0,1:T(8,128)S(1)} %get-tuple-element.88) | copy-start | bytes 12292
  101.4 11.4 %collective-permute-start = (bf16[2,3,1792]{2,0,1:T(2,128)(2,1)S(1)}, bf16[2,3,1792]{2,0,1:T(2,128)(2,1)S(1)}, u32[]{:S(2)}, u32[]{:S(2)}) collective-permute-start(bf16[2,3,1792]{2,0,1:T(2,128)(2,1)S(1)} %slice.325), channel_id=1, source_target_pairs={{0,4},{4,8},{8,12},{12,16},{16,20},{20,24},{24,28},{1,5},{5,9},{9,... | collective-permute-start | bytes 64520 | tf_op jit(solution)/shard_map/ppermute | solution.py:36
  111.7 262.6 %copy-start.105 = (f32[48]{0:T(128)}, f32[48]{0:T(128)S(1)}, u32[]{:S(2)}) copy-start(f32[48]{0:T(128)S(1)} %squeeze.17) | copy-start | bytes 580
  178.1 73.9 %copy-start.25 = (bf16[2,512,128]{2,0,1:T(2,128)(2,1)}, bf16[2,512,128]{2,0,1:T(2,128)(2,1)S(1)}, u32[]{:S(2)}) copy-start(bf16[2,512,128]{2,0,1:T(2,128)(2,1)S(1)} %get-tuple-element.80) | copy-start | bytes 786436
  190.5 27.1 %all-to-all-start = ((bf16[8,48,1152]{2,1,0:T(8,128)(2,1)}), bf16[8,48,1152]{2,1,0:T(8,128)(2,1)S(1)}, u32[]{:S(2)}, u32[]{:S(2)}) async-start(bf16[8,48,1152]{2,1,0:T(8,128)(2,1)} %bitcast.225), calls=%async_computation | async-start | bytes 1769472 | tf_op jit(solution)/shard_map/all_to_all | solution.py:46
  195.1 31.7 %all-gather.4.cloned.1.call-start = ((), (), s32[]{:S(2)}) async-start(), calls=%async_computation.6 | async-start | bytes 2949120 | tf_op jit(solution)/shard_map/all_gather | solution.py:106
  222.0 24.1 %all-to-all-start.1 = ((bf16[8,48,1024]{2,1,0:T(8,128)(2,1)}), bf16[8,48,1024]{2,1,0:T(8,128)(2,1)S(1)}, u32[]{:S(2)}, u32[]{:S(2)}) async-start(bf16[8,48,1024]{2,1,0:T(8,128)(2,1)} %fusion.262), calls=%async_computation.1 | async-start | bytes 1572864 | tf_op jit(solution)/shard_map/all_to_all | solution.py:53
  377.0 39.7 %all-to-all-start.2 = ((bf16[8,48,1152]{2,1,0:T(8,128)(2,1)}), bf16[8,48,1152]{2,1,0:T(8,128)(2,1)}, u32[]{:S(2)}, u32[]{:S(2)}) async-start(bf16[8,48,1152]{2,1,0:T(8,128)(2,1)} %bitcast.200), calls=%async_computation.2 | async-start | bytes 1769472 | tf_op jit(solution)/shard_map/all_to_all | solution.py:46
  423.8 25.2 %all-to-all-start.3 = ((bf16[8,48,1024]{2,1,0:T(8,128)(2,1)}), bf16[8,48,1024]{2,1,0:T(8,128)(2,1)S(1)}, u32[]{:S(2)}, u32[]{:S(2)}) async-start(bf16[8,48,1024]{2,1,0:T(8,128)(2,1)} %broadcast_dynamic-update-slice_fusion), calls=%async_computation.3 | async-start | bytes 1572864 | tf_op jit(solution)/shard_map/all_to_all | solution.py:53
  429.8 163.2 %reduce-scatter.3.cloned.1.call-start = ((), (), s32[]{:S(2)}) async-start(), calls=%async_computation.7 | async-start | bytes 5898240 | tf_op jit(solution)/shard_map/reduce_scatter | solution.py:315
  438.4 234.3 %all-reduce.11.cloned.1.call-start = ((), (), s32[]{:S(2)}) async-start(), calls=%async_computation.8 | async-start | bytes 2359296 | tf_op jit(solution)/shard_map/psum | solution.py:314
  584.7 7.5 collective-permute-start.1
  593.0 166.2 %reduce-scatter.5.cloned.1.call-start = ((), (), s32[]{:S(2)}) async-start(), calls=%async_computation.9 | async-start | bytes 6451200 | tf_op jit(solution)/shard_map/reduce_scatter | solution.py:322
  622.0 68.5 %copy-start.29 = (bf16[2,512,768]{2,1,0:T(8,128)(2,1)S(1)}, bf16[2,512,768]{2,1,0:T(8,128)(2,1)}, u32[]{:S(2)}) copy-start(bf16[2,512,768]{2,1,0:T(8,128)(2,1)} %param.10) | copy-start | bytes 4718596
  622.0 68.5 %copy-start.94 = (f32[768]{0:T(1024)S(1)}, f32[768]{0:T(1024)}, u32[]{:S(2)}) copy-start(f32[768]{0:T(1024)} %copy-done.93) | copy-start | bytes 9220
  708.9 137.4 %all-reduce.13.cloned.1.call-start = ((), (), s32[]{:S(2)}) async-start(), calls=%async_computation.10 | async-start | bytes 2580480 | tf_op jit(solution)/shard_map/psum | solution.py:321
  759.3 144.2 %all-reduce.15.cloned.1.call-start = ((), (), s32[]{:S(2)}) async-start(), calls=%async_computation.11 | async-start | bytes 4718592 | tf_op jit(solution)/shard_map/psum | solution.py:351
  813.3 176.1 %copy-start.11 = (f32[384,768]{1,0:T(8,128)}, f32[384,768]{1,0:T(8,128)S(1)}, u32[]{:S(2)}) copy-start(f32[384,768]{1,0:T(8,128)S(1)} %multiply_add_fusion.1) | copy-start | bytes 3538948
  818.7 184.5 %all-reduce.17.cloned.1.call-start = ((), (), s32[]{:S(2)}) async-start(), calls=%async_computation.12 | async-start | bytes 4718592 | tf_op jit(solution)/shard_map/psum | solution.py:355
  (100 other events, 846.8 us)
Sparse Core Ops, SparseCore 0:
  10.4 42.7 all-gather.5
  198.1 24.5 all-gather.3
  438.5 48.2 reduce-scatter.2
  593.1 79.5 all-reduce.10
  709.0 50.2 reduce-scatter.4
  763.1 83.1 all-reduce.12
  848.7 54.8 all-reduce.14
  947.4 55.7 all-reduce.16

commit v2 on v1

--- a/solution.py
+++ b/solution.py
@@ -118,10 +118,14 @@
     inv_rms = lax.rsqrt(jnp.mean(inputs * inputs, -1, keepdims=True) + EPSILON)
     scaled = inputs * inv_rms
     normed = (scaled * gain_in).astype(jnp.bfloat16)
-    projected = jnp.dot(normed, w_in_low, preferred_element_type=jnp.float32)
-    gate_pre = projected[..., :E]
-    conv_input = projected[..., E : E + CONV].astype(jnp.bfloat16)
-    step_raw = projected[..., E + CONV :]
+    w_gate, w_conv, w_step = (
+        w_in_low[:, :E],
+        w_in_low[:, E : E + CONV],
+        w_in_low[:, E + CONV :],
+    )
+    gate_pre = jnp.dot(normed, w_gate, preferred_element_type=jnp.float32)
+    conv_input = jnp.dot(normed, w_conv, preferred_element_type=jnp.float32).astype(jnp.bfloat16)
+    step_raw = jnp.dot(normed, w_step, preferred_element_type=jnp.float32)
     edge = from_behind(conv_input[:, local_rows - edge_rows :, :], "seq", 1)
     extended = jnp.concatenate([edge, conv_input], axis=1).astype(jnp.float32)
     doc_count = jnp.cumsum(starts, axis=1)
@@ -202,6 +206,15 @@
     result = (inputs + branch).astype(jnp.bfloat16)
     grad_w_out = jnp.einsum("ate,atd->ed", gated_low, cotangent, preferred_element_type=jnp.float32)
     grad_ghat = jnp.einsum("atd,ed->ate", cotangent, w_out_low, preferred_element_type=jnp.float32)
+    grad_w_out, grad_ghat = lax.optimization_barrier((grad_w_out, grad_ghat))
+    owner_out = lax.psum(
+        lax.psum_scatter(
+            grad_w_out.astype(jnp.bfloat16), "dp", scatter_dimension=0, tiled=True
+        ),
+        "seq",
+    ).astype(jnp.float32)
+    moment_out = MOMENTUM * out_moment + owner_out
+    gram_out = lax.psum(jnp.dot(moment_out.T, moment_out, precision=PRECISE), "dp")
     grad_gain_out = jnp.sum(grad_ghat * gated_hat, axis=(0, 1))
     grad_scaled_gate = grad_ghat * gain_out
     grad_gated = inv_gate * (
@@ -307,17 +320,20 @@
     grad_conv_in = jnp.concatenate(
         [grad_ext[:, edge_rows:local_rows], grad_ext[:, local_rows:] + grad_edge], axis=1
     )
-    grad_projected = jnp.concatenate([grad_gate, grad_conv_in, grad_arg], axis=-1).astype(
-        jnp.bfloat16
-    )
+    grad_conv_in, gram_out = lax.optimization_barrier(
+        (grad_conv_in.astype(jnp.bfloat16), gram_out)
+    )
+    grad_parts = (grad_gate.astype(jnp.bfloat16), grad_conv_in, grad_arg.astype(jnp.bfloat16))
     owners = lax.axis_size("dp")
-    owner_out = lax.psum(
-        lax.psum_scatter(grad_w_out, "dp", scatter_dimension=0, tiled=True), "seq"
-    )
-    grad_projected, owner_out = lax.optimization_barrier((grad_projected, owner_out))
-    grad_w_in = jnp.einsum(
-        "atj,atd->jd", grad_projected, normed, preferred_element_type=jnp.float32
-    ).astype(jnp.bfloat16)
+    grad_w_in = jnp.concatenate(
+        [
+            jnp.einsum("atj,atd->jd", part, normed, preferred_element_type=jnp.float32).astype(
+                jnp.bfloat16
+            )
+            for part in grad_parts
+        ],
+        axis=0,
+    )
     owner_in = lax.psum(
         lax.psum_scatter(
             grad_w_in.reshape(owners, IN // owners, D), "dp", scatter_dimension=0, tiled=False
@@ -325,8 +341,9 @@
         "seq",
     )
     owner_in = owner_in.astype(jnp.float32).T
-    grad_normed = jnp.einsum(
-        "atj,dj->atd", grad_projected, w_in_low, preferred_element_type=jnp.float32
+    grad_normed = sum(
+        jnp.einsum("atj,dj->atd", part, weight, preferred_element_type=jnp.float32)
+        for part, weight in zip(grad_parts, (w_gate, w_conv, w_step))
     )
     grad_gain_in = jnp.sum(grad_normed * scaled, axis=(0, 1))
     grad_scaled = grad_normed * gain_in
@@ -347,12 +364,8 @@
     summed_vec = lax.psum(grad_vec, ("seq", "dp"))
     vec_rows = vectors.shape[0]
     owner_vec = lax.dynamic_slice(summed_vec, (lax.axis_index("dp") * vec_rows,), (vec_rows,))
-    moment_out = MOMENTUM * out_moment + owner_out
-    gram_out = lax.psum(jnp.dot(moment_out.T, moment_out, precision=PRECISE), "dp")
     moment_in = MOMENTUM * in_moment + owner_in
-    gram_in = jnp.dot(moment_in, moment_in.T, precision=PRECISE)
-    gram_in, gram_out = lax.optimization_barrier((gram_in, gram_out))
-    gram_in = lax.psum(gram_in, "dp")
+    gram_in = lax.psum(jnp.dot(moment_in, moment_in.T, precision=PRECISE), "dp")
     factor_out = orthogonal_factor(gram_out)
     ortho_out = jnp.dot(moment_out, factor_out.T, precision=lax.Precision.HIGH)
     factor_in = orthogonal_factor(gram_in)

time: 1110 us -> 978 us (0.88)
  other arithmetic: 252 us -> 158 us
  local copies, waits for them, and re-layouts: 211 us -> 165 us
    psum x1, waiting for transfers between devices: 21.3 us -> 67.2 us  [per_device(): lax.psum(lax.psum_scatter(grad_w_in.reshape(owners, IN // owners, D), 'dp...]
    reduce_scatter x1, waiting for transfers between devices: 42.1 us -> 0.01 us  [per_device(): lax.psum_scatter(grad_w_in.reshape(owners, IN // owners, D), 'dp', scatte...]
    concatenate x1 -> x2, other arithmetic: 29 us -> 4.9 us  [the longest x1 2.82 us: per_device(): jnp.concatenate([jnp.einsum('atj,atd->jd', part, normed, preferred_elemen...]
    dot_general x1 -> x0, local copies, waits for them, and re-layouts: 21.3 us -> none  [per_device(): projected = jnp.dot(normed, w_in_low, preferred_element_type=jnp.float32)]
    optimization_barrier x1 -> x0, local copies, waits for them, and re-layouts: 17.9 us -> none  [per_device(): lax.optimization_barrier((grad_projected, owner_out))]
    reduce_sum x1, other arithmetic: 35.2 us -> 18.8 us  [per_device(): jnp.sum(grad_pre * extended[:, tap_index:tap_index + local_rows] * tap_ke...]
    reduce_sum x2, other arithmetic: 25.5 us -> 12.4 us  [per_device(): grad_skip = jnp.sum(grad_y * x_full, axis=(0, 1, 2, 4))]
    unnamed x241 -> x269, local copies, waits for them, and re-layouts: 21.8 us -> 33.9 us
  transfers between devices with their start and end apart: 14 -> 14, of which waited for: 9 -> 9; matrix products, arithmetic and copies ran while one was open for 31% -> 32% of each run, Pallas kernels for 0% -> 0%
where the time goes in v2:
time: 978 us; the launch traced here: 970 us
  matrix products  313 us (32%)
  waiting for transfers between devices  235 us (24%)
  local copies, waits for them, and re-layouts  165 us (17%)
  other arithmetic  158 us (16%)
  blocking collectives  53.5 us (5%)
  starting transfers between devices  26.3 us (3%)
  between operations  18.3 us (2%)
    psum x1, waiting for transfers between devices, per_device(): lax.psum(lax.psum_scatter(grad_w_in.reshape(owners, IN // owners, D), 'dp...  67.2 us
    psum x1, waiting for transfers between devices, per_device(): lax.psum(lax.psum_scatter(grad_w_out.astype(jnp.bfloat16), 'dp', scatter_...  53.1 us
    another operation x19, other arithmetic  48.8 us
    psum x1, waiting for transfers between devices, per_device(): lax.psum(jnp.dot(moment_out.T, moment_out, precision=PRECISE), 'dp')  46.6 us
    dot_general x10, matrix products, orthogonal_factor(): square = jnp.dot(gram, gram, precision=precision)  45.4 us
    psum x1, blocking collectives, per_device(): summed_vec = lax.psum(grad_vec, ('seq', 'dp'))  40.7 us
    dot_general x8, matrix products, orthogonal_factor(): jnp.dot(poly, factor, precision=precision)  39.4 us
    dot_general x8, matrix products, orthogonal_factor(): jnp.dot(poly, gram, precision=precision)  39.2 us
  transfers between devices with their start and end apart: 14, of which 9 were waited for; matrix products, arithmetic and copies ran while one was open for 32% of the time, Pallas kernels for 0%

profile of v2, /device:TPU:0, one launch (start us, length us, event | category | flops | bytes accessed | tf_op | source)
XLA Modules:
  0.0 970.0 jit_solution(3642719966226447684)
XLA Ops:
  12.0 12.9 %all-reduce.5 = bf16[11336]{0:T(1024)(128)(2,1)S(1)} all-reduce(bf16[11336]{0:T(1024)(128)(2,1)S(1)} %dynamic-update-slice), channel_id=1, replica_groups=mesh['seq'=8,'dp'=4] {'dp'}, use_global_device_ids=true, to_apply=%add.5 | all-reduce | flops 11336 | bytes 45344
  28.9 24.3 %all-gather.6.cloned.1.call-done = bf16[4,838,768]{2,1,0:T(8,128)(2,1)} async-done(((bf16[1,838,768]{2,1,0:T(8,128)(2,1)}), bf16[4,838,768]{2,1,0:T(8,128)(2,1)}) %all-gather.6.cloned.1.call-update) | async-done | bytes 5148688 | tf_op jit(solution)/shard_map/all_gather | solution.py:105
  59.3 7.8 copy.227
  91.6 18.7 %fusion.382 = (bf16[2,512,1792]{2,1,0:T(8,128)(2,1)S(1)}, f32[2,512,1792]{2,1,0:T(8,128)}, f32[2,512,1792]{2,1,0:T(8,128)}) fusion(f32[1792]{0:T(1024)S(1)} %get-tuple-element.98, f32[2,515,1792]{2,1,0:T(8,128)} %maximum_convert_fusion, f32[2,512]{1,0:T(2,128)S(1)} %get-tuple-element.103, f32[1792]{0:T(1024)S(1)} %get-tuple-element.97, ...), kind=kLoop, calls=%fused_computation.499 | loop fusion | flops 29360128 | bytes 47758336 | tf_op jit(solution)/shard_map/convert.24
  116.3 10.0 %reshape.712 = f32[2,2,256,24,64]{4,3,2,1,0:T(8,128)} reshape(f32[2,512,1536]{2,1,0:T(8,128)} %slice.334) | data formatting | bytes 12582912 | tf_op jit(solution)/shard_map/reshape | solution.py:154
  126.3 9.7 %copy.229 = f32[2,2,256,24,64]{2,4,3,1,0:T(8,128)} copy(f32[2,2,256,24,64]{4,3,2,1,0:T(8,128)} %reshape.712) | data formatting | bytes 12582912 | tf_op jit(solution)/shard_map/reshape | solution.py:154
  157.9 20.1 %all-to-all-done = bf16[8,48,1152]{2,1,0:T(8,128)(2,1)S(1)} async-done(((bf16[8,48,1152]{2,1,0:T(8,128)(2,1)}), bf16[8,48,1152]{2,1,0:T(8,128)(2,1)S(1)}, u32[]{:S(2)}, u32[]{:S(2)}) %all-to-all-start) | async-done | bytes 884768 | tf_op jit(solution)/shard_map/all_to_all | solution.py:46
  196.5 10.9 %all-to-all-done.1 = bf16[8,48,1024]{2,1,0:T(8,128)(2,1)S(1)} async-done(((bf16[8,48,1024]{2,1,0:T(8,128)(2,1)}), bf16[8,48,1024]{2,1,0:T(8,128)(2,1)S(1)}, u32[]{:S(2)}, u32[]{:S(2)}) %all-to-all-start.1) | async-done | bytes 786464 | tf_op jit(solution)/shard_map/all_to_all | solution.py:53
  218.4 9.2 fusion.12
  227.5 9.8 %copy.283 = f32[2,2,256,24,64]{4,3,2,1,0:T(8,128)} copy(f32[2,2,256,24,64]{2,4,3,1,0:T(8,128)} %fusion.12) | data formatting | bytes 12582912 | tf_op jit(solution)/shard_map/reshape | solution.py:199
  237.3 11.2 %reshape.713 = f32[2,512,1536]{2,1,0:T(8,128)} reshape(f32[2,2,256,24,64]{4,3,2,1,0:T(8,128)} %copy.283) | data formatting | bytes 12582912 | tf_op jit(solution)/shard_map/reshape | solution.py:199
  248.6 8.4 multiply_reduce_fusion.10
  272.3 11.7 %multiply_reduce_fusion.6 = (f32[1536]{0:T(1024)}, f32[2,512,1536]{2,1,0:T(8,128)}, bf16[2,512,1536]{2,1,0:T(8,128)(2,1)}) fusion(f32[2,512,1792]{2,1,0:T(8,128)} %get-tuple-element.69, f32[2,512,1536]{2,1,0:T(8,128)} %get-tuple-element.107, f32[2,512]{1,0:T(2,128)S(1)} %broadcast_multiply_fusion.2, f32[2,512,1536]{2,1,0:T(8,128)S(1)} %bitcast.255, ...), kind=kLoop, calls=%fused_computation.40 | loop fusion | flops 29882880 | bytes 40914944 | tf_op jit(solution)/shard_map/reduce_sum | solution.py:229
  290.6 8.2 reshape.679
  322.1 20.6 %fusion.2 = (f32[2,2,24,256]{3,2,1,0:T(8,128)}, f32[2,2,24,256]{3,2,1,0:T(8,128)}, f32[2,2,24,256]{3,2,1,0:T(8,128)}, bf16[2,2,256,256]{3,2,1,0:T(8,128)(2,1)}) fusion(f32[2,2,24,256]{3,2,1,0:T(8,128)} %copy.234, f32[2,2,24,256]{3,2,1,0:T(8,128)} %get-tuple-element.86, f32[2,2,256,256]{3,2,1,0:T(8,128)} %fusion.393, ...), kind=kOutput, calls=%fused_computation.6 | convolution fusion | flops 888332288 | bytes 11763712 | tf_op jit(solution)/shard_map/abthp,abshp->abhts/dot_general | solution.py:231
  368.2 6.9 multiply_reduce_fusion.8
  400.2 9.2 fusion.11
  423.2 9.8 %copy.279 = f32[2,2,256,24,64]{4,3,2,1,0:T(8,128)} copy(f32[2,2,256,24,64]{2,4,3,1,0:T(8,128)} %fusion.11) | data formatting | bytes 12582912 | tf_op jit(solution)/shard_map/reshape | solution.py:294
  433.0 11.3 %reshape.711 = f32[2,512,1536]{2,1,0:T(8,128)} reshape(f32[2,2,256,24,64]{4,3,2,1,0:T(8,128)} %copy.279) | data formatting | bytes 12582912 | tf_op jit(solution)/shard_map/reshape | solution.py:294
  449.2 18.8 %multiply_reduce_fusion.5 = (f32[1792]{0:T(1024)}, f32[1792]{0:T(1024)}, f32[1792]{0:T(1024)}, f32[1792]{0:T(1024)}, f32[1792]{0:T(1024)S(1)}, /*index=5*/f32[2,512,1792]{2,1,0:T(8,128)S(1)}) fusion(f32[2,515,1792]{2,1,0:T(8,128)} %maximum_convert_fusion, f32[2,512]{1,0:T(2,128)S(1)} %copy-done.84, f32[2,512]{1,0:T(2,128)S(1)} %copy-done.88, ...), kind=kLoop, calls=%fused_computation.27 | loop fusion | flops 40361216 | bytes 51428352 | tf_op jit(solution)/shard_map/reduce_sum | solution.py:304
  468.1 10.8 %multiply_multiply_fusion.3 = (f32[2,512,1792]{2,1,0:T(8,128)}, f32[2,512,1792]{2,1,0:T(8,128)}, f32[2,512,1792]{2,1,0:T(8,128)}, f32[2,512,1792]{2,1,0:T(8,128)}) fusion(f32[2,512,1792]{2,1,0:T(8,128)S(1)} %get-tuple-element.53, f32[2,512]{1,0:T(2,128)S(1)} %copy-done.84, f32[1792]{0:T(1024)S(1)} %copy-done.74, f32[1792]{0:T(1024)S(1)} %copy-done.80, ...), kind=kLoop, calls=%fused_computation.30 | loop fusion | flops 12845056 | bytes 36741120 | tf_op jit(solution)/shard_map/mul | solution.py:314
  479.7 14.0 %fusion.380 = (bf16[2,515,1792]{2,1,0:T(8,128)(2,1)S(1)}, f32[2,515,1792]{2,1,0:T(8,128)}) fusion(f32[2,512,1792]{2,1,0:T(8,128)} %get-tuple-element.73, f32[2,512,1792]{2,1,0:T(8,128)} %get-tuple-element.74, f32[2,512,1792]{2,1,0:T(8,128)} %get-tuple-element.75, f32[2,512,1792]{2,1,0:T(8,128)} %get-tuple-element.72), kind=kLoop, calls=%fused_computation.498 | loop fusion | flops 7383040 | bytes 40434688 | tf_op jit(solution)/shard_map/convert.13
  496.9 53.1 %all-reduce.11.cloned.1.call-done = bf16[384,768]{1,0:T(8,128)(2,1)} async-done(((bf16[384,768]{1,0:T(8,128)(2,1)}), bf16[384,768]{1,0:T(8,128)(2,1)}) %all-reduce.11.cloned.1.call-update) | async-done | bytes 589840 | tf_op jit(solution)/shard_map/psum | solution.py:210
  564.7 46.6 %all-reduce.13.cloned.1.call-done = f32[768,768]{1,0:T(8,128)} async-done(((f32[768,768]{1,0:T(8,128)}), f32[768,768]{1,0:T(8,128)}) %all-reduce.13.cloned.1.call-update) | async-done | bytes 2359312 | tf_op jit(solution)/shard_map/psum | solution.py:217
  627.2 7.0 fusion.112
  634.3 7.6 fusion.25
  708.6 6.7 fusion.78
  723.9 7.2 fusion.51
  740.0 67.2 %all-reduce.15.cloned.1.call-done = bf16[768,838]{0,1:T(8,128)(2,1)} async-done(((bf16[768,838]{0,1:T(8,128)(2,1)}), bf16[768,838]{0,1:T(8,128)(2,1)}) %all-reduce.15.cloned.1.call-update) | async-done | bytes 1287184 | tf_op jit(solution)/shard_map/psum | solution.py:337
  811.1 9.5 fusion.395
  821.4 40.7 %psum.39 = f32[11336]{0:T(1024)S(1)} all-reduce(f32[11336]{0:T(1024)S(1)} %concatenate.39), channel_id=1, replica_groups=mesh['seq'=8,'dp'=4] {'seq','dp'}, use_global_device_ids=true, to_apply=%region_40.41 | all-reduce | flops 11336 | bytes 90688 | tf_op jit(solution)/shard_map/psum | solution.py:364
  886.1 6.8 fusion.110
  (490 shorter events, 424.9 us)
Async XLA Ops:
  7.2 46.0 %all-gather.6.cloned.1.call-start = ((), (), s32[]{:S(2)}) async-start(), calls=%async_computation.13 | async-start | bytes 6451200 | tf_op jit(solution)/shard_map/all_gather | solution.py:105
  24.8 350.2 %copy-start.92 = (f32[768]{0:T(1024)}, f32[768]{0:T(1024)S(1)}, u32[]{:S(2)}) copy-start(f32[768]{0:T(1024)S(1)} %slice.322) | copy-start | bytes 9220
  28.4 50.7 %copy-start.113 = (f32[2,2]{1,0:T(2,128)}, f32[2,2]{1,0:T(2,128)S(1)}, u32[]{:S(2)}) copy-start(f32[2,2]{1,0:T(2,128)S(1)} %fusion.265) | copy-start | bytes 52
  28.6 44.9 %copy-start.119 = (f32[24]{0:T(128)}, f32[24]{0:T(128)S(1)}, u32[]{:S(2)}) copy-start(f32[24]{0:T(128)S(1)} %fusion.266) | copy-start | bytes 292
  28.6 346.5 %copy-start.94 = (f32[2,512]{1,0:T(2,128)}, f32[2,512]{1,0:T(2,128)S(1)}, u32[]{:S(2)}) copy-start(f32[2,512]{1,0:T(2,128)S(1)} %add_rsqrt_fusion.1) | copy-start | bytes 12292
  28.7 55.8 %copy-start.96 = (f32[2,2,256]{2,1,0:T(2,128)}, f32[2,2,256]{2,1,0:T(2,128)S(1)}, u32[]{:S(2)}) copy-start(f32[2,2,256]{2,1,0:T(2,128)S(1)} %get-tuple-element.100) | copy-start | bytes 12292
  28.7 55.8 %copy-start.98 = (f32[2,2,256]{2,1,0:T(2,128)}, f32[2,2,256]{2,1,0:T(2,128)S(1)}, u32[]{:S(2)}) copy-start(f32[2,2,256]{2,1,0:T(2,128)S(1)} %get-tuple-element.99) | copy-start | bytes 12292
  28.8 62.8 %copy-start.83 = (f32[2,512]{1,0:T(2,128)}, f32[2,512]{1,0:T(2,128)S(1)}, u32[]{:S(2)}) copy-start(f32[2,512]{1,0:T(2,128)S(1)} %get-tuple-element.101) | copy-start | bytes 12292
  28.8 62.8 %copy-start.85 = (f32[2,512]{1,0:T(2,128)}, f32[2,512]{1,0:T(2,128)S(1)}, u32[]{:S(2)}) copy-start(f32[2,512]{1,0:T(2,128)S(1)} %get-tuple-element.102) | copy-start | bytes 12292
  28.8 62.8 %copy-start.87 = (f32[2,512]{1,0:T(2,128)}, f32[2,512]{1,0:T(2,128)S(1)}, u32[]{:S(2)}) copy-start(f32[2,512]{1,0:T(2,128)S(1)} %get-tuple-element.103) | copy-start | bytes 12292
  28.8 62.7 %copy-start.73 = (f32[1792]{0:T(1024)}, f32[1792]{0:T(1024)S(1)}, u32[]{:S(2)}) copy-start(f32[1792]{0:T(1024)S(1)} %get-tuple-element.95) | copy-start | bytes 21508
  28.9 62.7 %copy-start.75 = (f32[1792]{0:T(1024)}, f32[1792]{0:T(1024)S(1)}, u32[]{:S(2)}) copy-start(f32[1792]{0:T(1024)S(1)} %get-tuple-element.96) | copy-start | bytes 21508
  28.9 62.7 %copy-start.77 = (f32[1792]{0:T(1024)}, f32[1792]{0:T(1024)S(1)}, u32[]{:S(2)}) copy-start(f32[1792]{0:T(1024)S(1)} %get-tuple-element.97) | copy-start | bytes 21508
  28.9 62.7 %copy-start.79 = (f32[1792]{0:T(1024)}, f32[1792]{0:T(1024)S(1)}, u32[]{:S(2)}) copy-start(f32[1792]{0:T(1024)S(1)} %get-tuple-element.98) | copy-start | bytes 21508
  80.9 5.0 collective-permute-start
  84.6 51.4 %copy-start.43 = (f32[2,2,256,24]{2,3,1,0:T(8,128)}, f32[2,2,256,24]{2,3,1,0:T(8,128)S(1)}, u32[]{:S(2)}) copy-start(f32[2,2,256,24]{2,3,1,0:T(8,128)S(1)} %get-tuple-element.89) | copy-start | bytes 294916
  110.4 102.8 %copy-start.31 = (bf16[2,512,128]{2,1,0:T(8,128)(2,1)}, bf16[2,512,128]{2,1,0:T(8,128)(2,1)S(1)}, u32[]{:S(2)}) copy-start(bf16[2,512,128]{2,1,0:T(8,128)(2,1)S(1)} %get-tuple-element.77) | copy-start | bytes 786436
  150.0 28.1 %all-to-all-start = ((bf16[8,48,1152]{2,1,0:T(8,128)(2,1)}), bf16[8,48,1152]{2,1,0:T(8,128)(2,1)S(1)}, u32[]{:S(2)}, u32[]{:S(2)}) async-start(bf16[8,48,1152]{2,1,0:T(8,128)(2,1)} %bitcast.245), calls=%async_computation | async-start | bytes 1769472 | tf_op jit(solution)/shard_map/all_to_all | solution.py:46
  156.3 32.0 %all-gather.4.cloned.1.call-start = ((), (), s32[]{:S(2)}) async-start(), calls=%async_computation.6 | async-start | bytes 2949120 | tf_op jit(solution)/shard_map/all_gather | solution.py:106
  183.5 23.9 %all-to-all-start.1 = ((bf16[8,48,1024]{2,1,0:T(8,128)(2,1)}), bf16[8,48,1024]{2,1,0:T(8,128)(2,1)S(1)}, u32[]{:S(2)}, u32[]{:S(2)}) async-start(bf16[8,48,1024]{2,1,0:T(8,128)(2,1)} %fusion.253), calls=%async_computation.1 | async-start | bytes 1572864 | tf_op jit(solution)/shard_map/all_to_all | solution.py:53
  187.3 82.9 %copy-start.81 = (f32[1536]{0:T(1024)}, f32[1536]{0:T(1024)S(1)}, u32[]{:S(2)}) copy-start(f32[1536]{0:T(1024)S(1)} %slice.366) | copy-start | bytes 18436
  317.9 34.8 %all-to-all-start.2 = ((bf16[8,48,1152]{2,1,0:T(8,128)(2,1)}), bf16[8,48,1152]{2,1,0:T(8,128)(2,1)}, u32[]{:S(2)}, u32[]{:S(2)}) async-start(bf16[8,48,1152]{2,1,0:T(8,128)(2,1)} %bitcast.271), calls=%async_computation.2 | async-start | bytes 1769472 | tf_op jit(solution)/shard_map/all_to_all | solution.py:46
  322.1 156.8 %reduce-scatter.3.cloned.1.call-start = ((), (), s32[]{:S(2)}) async-start(), calls=%async_computation.7 | async-start | bytes 2949120 | tf_op jit(solution)/shard_map/reduce_scatter | solution.py:211
  359.9 25.1 %all-to-all-start.3 = ((bf16[8,48,1024]{2,1,0:T(8,128)(2,1)}), bf16[8,48,1024]{2,1,0:T(8,128)(2,1)}, u32[]{:S(2)}, u32[]{:S(2)}) async-start(bf16[8,48,1024]{2,1,0:T(8,128)(2,1)} %broadcast_dynamic-update-slice_fusion), calls=%async_computation.3 | async-start | bytes 1572864 | tf_op jit(solution)/shard_map/all_to_all | solution.py:53
  365.8 184.2 %all-reduce.11.cloned.1.call-start = ((), (), s32[]{:S(2)}) async-start(), calls=%async_computation.8 | async-start | bytes 1179648 | tf_op jit(solution)/shard_map/psum | solution.py:210
  478.9 132.4 %all-reduce.13.cloned.1.call-start = ((), (), s32[]{:S(2)}) async-start(), calls=%async_computation.9 | async-start | bytes 4718592 | tf_op jit(solution)/shard_map/psum | solution.py:217
  479.7 70.3 %copy-start.48 = (f32[384,768]{1,0:T(8,128)S(1)}, f32[384,768]{1,0:T(8,128)}, u32[]{:S(2)}) copy-start(f32[384,768]{1,0:T(8,128)} %param.17) | copy-start | bytes 3538948
  495.6 66.1 %collective-permute-start.1 = (bf16[2,3,1792]{2,1,0:T(4,128)(2,1)S(1)}, bf16[2,3,1792]{2,1,0:T(4,128)(2,1)S(1)}, u32[]{:S(2)}, u32[]{:S(2)}) collective-permute-start(bf16[2,3,1792]{2,1,0:T(4,128)(2,1)S(1)} %slice.385), channel_id=1, source_target_pairs={{4,0},{8,4},{12,8},{16,12},{20,16},{24,20},{28,24},{5,1},{9,5},{13... | collective-permute-start | bytes 64520 | tf_op jit(solution)/shard_map/ppermute | solution.py:36
  551.2 311.7 %copy-start.12 = (f32[384,768]{1,0:T(8,128)}, f32[384,768]{1,0:T(8,128)S(1)}, u32[]{:S(2)}) copy-start(f32[384,768]{1,0:T(8,128)S(1)} %convert_add_fusion.2) | copy-start | bytes 3538948
  556.6 166.7 %reduce-scatter.5.cloned.1.call-start = ((), (), s32[]{:S(2)}) async-start(), calls=%async_computation.10 | async-start | bytes 6451200 | tf_op jit(solution)/shard_map/reduce_scatter | solution.py:338
  625.8 181.4 %all-reduce.15.cloned.1.call-start = ((), (), s32[]{:S(2)}) async-start(), calls=%async_computation.11 | async-start | bytes 2580480 | tf_op jit(solution)/shard_map/psum | solution.py:337
  723.4 153.3 %all-reduce.17.cloned.1.call-start = ((), (), s32[]{:S(2)}) async-start(), calls=%async_computation.12 | async-start | bytes 4718592 | tf_op jit(solution)/shard_map/psum | solution.py:368
  (112 other events, 871.9 us)
Sparse Core Ops, SparseCore 0:
  10.4 42.7 all-gather.5
  159.3 24.5 all-gather.3
  347.6 33.4 reduce-scatter.2
  479.0 70.9 all-reduce.10
  556.7 54.5 all-reduce.12
  625.9 50.9 reduce-scatter.4
  723.5 83.6 all-reduce.14
  820.8 55.8 all-reduce.16
